TPU v7x, 32 devices: a whole 2x2x4 slice. The times are simulated.
32 devices in a mesh: grp: 2 (over y), batch: 16 (over z, x, core).
Axes of the slice: x: 2, y: 2, z: 4, core: 2. Of those that a mesh axis runs over, the one named last changes fastest.
Arguments:
- tokens: bfloat16 [32768, 768], P(('grp', 'batch')), may hold values from -6 to 6
- buckets: int32 [64], P(('grp', 'batch')), may hold values from 0 to 2, as said below
- lengths: int32 [64, 16], P(('grp', 'batch')), may hold values from 0 to 256, as said below
- positives: int32 [512], replicated, may hold values from 0 to 95
- w_query: bfloat16 [768, 768], replicated, may hold values from -0.21875 to 0.21875
- b_query: float32 [768], replicated, may hold values from -3 to 3
- w_key: bfloat16 [768, 768], replicated, may hold values from -0.21875 to 0.21875
- w_value: bfloat16 [768, 768], replicated, may hold values from -0.21875 to 0.21875
- b_value: float32 [768], replicated, may hold values from -3 to 3
- w_out: bfloat16 [768, 768], replicated, may hold values from -1.25 to 1.25
- b_out: float32 [768], replicated, may hold values from -3 to 3
- gain_attn: float32 [768], replicated, may hold values from 0.25 to 1.75
- shift_attn: float32 [768], replicated, may hold values from -1.2 to 1.2
- w_in: bfloat16 [768, 3072], replicated, may hold values from -0.21875 to 0.21875
- b_in: float32 [3072], replicated, may hold values from -3 to 3
- w_back: bfloat16 [3072, 768], replicated, may hold values from -0.109375 to 0.109375
- b_back: float32 [768], replicated, may hold values from -3 to 3
- gain_ffn: float32 [768], replicated, may hold values from 0.25 to 1.75
- shift_ffn: float32 [768], replicated, may hold values from -1.2 to 1.2
Outputs:
- encoded: bfloat16 [32768, 768], P(('grp', 'batch'))
- grad_tokens: float32 [32768, 768], P(('grp', 'batch'))
- grad_w_query: float32 [768, 768], P('batch')
- grad_b_query: float32 [768], P('batch')
- grad_w_key: float32 [768, 768], P('batch')
- grad_w_value: float32 [768, 768], P('batch')
- grad_b_value: float32 [768], P('batch')
- grad_w_out: float32 [768, 768], P('batch')
- grad_b_out: float32 [768], P('batch')
- grad_gain_attn: float32 [768], P('batch')
- grad_shift_attn: float32 [768], P('batch')
- grad_w_in: float32 [768, 3072], P('batch')
- grad_b_in: float32 [3072], P('batch')
- grad_w_back: float32 [3072, 768], P('batch')
- grad_b_back: float32 [768], P('batch')
- grad_gain_ffn: float32 [768], P('batch')
- grad_shift_ffn: float32 [768], P('batch')
Inputs may be any that keep to these rules, and one draw needn't show every extreme that they name: `buckets`: blocks of the devices of grp index 0 are 0. On every other device the blocks come in pairs (blocks 0 and 1, 2 and 3, ...) holding one 1 and one 2. lengths[b, s] is 0 where s times the slot size of block b is 512 or more, and otherwise 1 to that slot size; in every block one slot is full.
All inputs are finite; a program needn't handle non-finite values.
Results may differ from a plain program's by a relative error of at most 0.014.
Values may be sent and summed in bfloat16 or wider, within the bound.
A program may use at most 192 MiB of HBM per device.

v0:
```python
import jax
import jax.numpy as jnp
from jax import lax
from jax.sharding import PartitionSpec as P

H = 12
HD = 64
QLEN = 32
SHORT = 128
LONG = 256
BLK = 512
SLOTS_BLK = 16
PAS_DEV = 6


norm_epsilon = 1e-06


def matmul(left, right):
    return jnp.dot(left, right, preferred_element_type=jnp.float32)


def matmul_tn(left, right):
    return lax.dot_general(
        left, right, (((0,), (0,)), ((), ())), preferred_element_type=jnp.float32
    )


def matmul_nt(left, right):
    return lax.dot_general(
        left, right, (((1,), (1,)), ((), ())), preferred_element_type=jnp.float32
    )


def gelu_exact(values):
    return jax.nn.gelu(values, approximate=False)


def slot_sizes(buckets):
    return jnp.where(buckets == 0, QLEN, jnp.where(buckets == 1, SHORT, LONG)).astype(jnp.int32)


def candidates(buckets):
    sizes_here = slot_sizes(buckets)
    slot_index = jnp.arange(SLOTS_BLK, dtype=jnp.int32)
    starts = slot_index[None, :] * sizes_here[:, None]
    inside = starts < BLK
    return (jnp.where(inside, starts, 0), inside)


def compact_order(inside):
    flattened = inside.reshape(-1)
    places = jnp.arange(flattened.shape[0], dtype=jnp.int32)
    return jnp.argsort(jnp.where(flattened, places, places + flattened.shape[0]))


def block_mask(bucket, slot_lengths):
    width_slot = slot_sizes(bucket)
    places = jnp.arange(BLK, dtype=jnp.int32)
    segment = places // width_slot
    within = places - segment * width_slot
    slot_index = jnp.arange(SLOTS_BLK, dtype=jnp.int32)
    limits = jnp.sum(
        jnp.where(segment[:, None] == slot_index[None, :], slot_lengths[None, :], 0), axis=1
    )
    return (segment[:, None] == segment[None, :]) & (within < limits)[None, :]


def layer_norm(hidden, scale_vec, shift_vec):
    center = hidden - jnp.mean(hidden, axis=-1, keepdims=True)
    spread = jnp.mean(center * center, axis=-1, keepdims=True)
    return center * lax.rsqrt(spread + norm_epsilon) * scale_vec + shift_vec


def rank_gradient(query_block, passages, picked, score_scale):
    scores = matmul_nt(query_block, passages) * score_scale
    targets = (jnp.arange(passages.shape[0], dtype=jnp.int32)[None, :] == picked[:, None]).astype(
        jnp.float32
    )
    return (jax.nn.softmax(scores, axis=1) - targets).astype(jnp.bfloat16)


def shards(
    tokens,
    buckets,
    lengths,
    positives,
    w_query,
    b_query,
    w_key,
    w_value,
    b_value,
    w_out,
    b_out,
    gain_attn,
    shift_attn,
    w_in,
    b_in,
    w_back,
    b_back,
    gain_ffn,
    shift_ffn,
):
    tok_rows = tokens.shape[0]
    width = tokens.shape[1]
    blocks = tok_rows // BLK
    block_shape = (blocks, BLK, H, HD)
    head_scale = HD ** (-0.5)
    inputs = tokens.astype(jnp.float32)
    query_rows = (matmul(tokens, w_query) + b_query).astype(jnp.bfloat16)
    key_rows = matmul(tokens, w_key).astype(jnp.bfloat16)
    value_rows = (matmul(tokens, w_value) + b_value).astype(jnp.bfloat16)

    def attend(packed):
        query_blk, key_blk, value_blk, bucket, slot_lengths = packed
        scores = (
            jnp.einsum("qhd,khd->hqk", query_blk, key_blk, preferred_element_type=jnp.float32)
            * head_scale
        )
        scores = jnp.where(block_mask(bucket, slot_lengths)[None], scores, -1e30)
        highest = jnp.max(scores, axis=-1, keepdims=True)
        raised = jnp.exp(scores - highest)
        row_totals = jnp.sum(raised, axis=-1, keepdims=True)
        weights = (raised / row_totals).astype(jnp.bfloat16)
        mixed_blk = jnp.einsum(
            "hqk,khd->qhd", weights, value_blk, preferred_element_type=jnp.float32
        )
        return (mixed_blk.astype(jnp.bfloat16), (highest + jnp.log(row_totals))[..., 0])

    mixed_heads, log_totals = lax.map(
        attend,
        (
            query_rows.reshape(block_shape),
            key_rows.reshape(block_shape),
            value_rows.reshape(block_shape),
            buckets,
            lengths,
        ),
    )
    mixed_heads = mixed_heads.reshape(tok_rows, width)
    hidden_one = inputs + matmul(mixed_heads, w_out) + b_out
    normed = layer_norm(hidden_one, gain_attn, shift_attn)
    normed_low = normed.astype(jnp.bfloat16)
    hidden_pre = matmul(normed_low, w_in) + b_in
    active = gelu_exact(hidden_pre).astype(jnp.bfloat16)
    hidden_two = normed + matmul(active, w_back) + b_back
    output = layer_norm(hidden_two, gain_ffn, shift_ffn)
    encoded = output.astype(jnp.bfloat16)
    slot_starts, inside = candidates(buckets)
    cand_rows = (slot_starts + BLK * jnp.arange(blocks, dtype=jnp.int32)[:, None]).reshape(-1)
    order_index = compact_order(inside)
    inverse_index = jnp.argsort(order_index)
    cls_count = cand_rows.shape[0]
    cls_mine = output[cand_rows[order_index]].astype(jnp.bfloat16)
    groups = lax.axis_size("grp")
    members = lax.axis_size("batch")
    group_here = lax.axis_index("grp")
    member_here = lax.axis_index("batch")
    gathered = lax.all_gather(cls_mine, ("grp", "batch"), axis=0, tiled=True).reshape(
        groups, members, cls_count, width
    )
    queries = gathered[0].reshape(members * cls_count, width)
    passages = gathered[1:, :, :PAS_DEV].reshape((groups - 1) * members * PAS_DEV, width)
    score_scale = width ** (-0.5)
    query_share = cls_count // groups
    first_query = member_here * cls_count + group_here * query_share
    own_queries = lax.dynamic_slice_in_dim(queries, first_query, query_share, 0)
    own_picked = lax.dynamic_slice_in_dim(positives, first_query, query_share, 0)
    rank_grad = rank_gradient(own_queries, passages, own_picked, score_scale)
    query_part = matmul(rank_grad, passages) * score_scale
    query_rows_grad = lax.all_gather(query_part, "grp", axis=0, tiled=True)
    passage_terms = jnp.concatenate(
        [
            jnp.zeros((members * PAS_DEV, width), jnp.float32),
            matmul_tn(rank_grad, own_queries) * score_scale,
        ],
        axis=0,
    )
    passage_rows_grad = lax.psum_scatter(
        passage_terms, ("grp", "batch"), scatter_dimension=0, tiled=True
    )
    padded_passage = jnp.pad(passage_rows_grad, ((0, cls_count - PAS_DEV), (0, 0)))
    cls_grad = jnp.where(group_here == 0, query_rows_grad, padded_passage)
    output_grad = cls_grad[inverse_index]
    kept_two, pull_two = jax.vjp(layer_norm, hidden_two[cand_rows], gain_ffn, shift_ffn)
    two_grad, gain_ffn_grad, shift_ffn_grad = pull_two(output_grad)
    branch_grad = two_grad.astype(jnp.bfloat16)
    b_back_grad = jnp.sum(branch_grad.astype(jnp.float32), axis=0)
    w_back_grad = matmul_tn(active[cand_rows], branch_grad)
    kept_gelu, pull_gelu = jax.vjp(gelu_exact, hidden_pre[cand_rows])
    pre_grad = pull_gelu(matmul_nt(branch_grad, w_back))[0].astype(jnp.bfloat16)
    b_in_grad = jnp.sum(pre_grad.astype(jnp.float32), axis=0)
    w_in_grad = matmul_tn(normed_low[cand_rows], pre_grad)
    normed_grad = two_grad + matmul_nt(pre_grad, w_in)
    kept_one, pull_one = jax.vjp(layer_norm, hidden_one[cand_rows], gain_attn, shift_attn)
    one_grad, gain_attn_grad, shift_attn_grad = pull_one(normed_grad)
    attn_grad = one_grad.astype(jnp.bfloat16)
    b_out_grad = jnp.sum(attn_grad.astype(jnp.float32), axis=0)
    w_out_grad = matmul_tn(mixed_heads[cand_rows], attn_grad)
    mixed_grad = matmul_nt(attn_grad, w_out).astype(jnp.bfloat16)
    slots_block = slot_starts.shape[1]
    row_shape = (blocks, slots_block, H, HD)
    query_cls = query_rows[cand_rows].reshape(row_shape)
    mixed_cls = mixed_grad.reshape(row_shape)
    log_cls = jnp.take_along_axis(
        log_totals, jnp.broadcast_to(slot_starts[:, None, :], (blocks, H, slots_block)), axis=2
    )

    def attend_back(packed):
        query_blk, key_blk, value_blk, grad_blk, log_blk, bucket, slot_lengths, start_blk = packed
        visible = block_mask(bucket, slot_lengths)[start_blk]
        scores_blk = (
            jnp.einsum("shd,khd->hsk", query_blk, key_blk, preferred_element_type=jnp.float32)
            * head_scale
        )
        scores_blk = jnp.where(visible[None], scores_blk, -1e30)
        weights = jnp.exp(scores_blk - log_blk[..., None])
        value_back = jnp.einsum(
            "hsk,shd->khd",
            weights.astype(jnp.bfloat16),
            grad_blk,
            preferred_element_type=jnp.float32,
        )
        weight_grad = jnp.einsum(
            "shd,khd->hsk", grad_blk, value_blk, preferred_element_type=jnp.float32
        )
        score_back = (
            weights * (weight_grad - jnp.sum(weights * weight_grad, axis=-1, keepdims=True))
        ).astype(jnp.bfloat16)
        query_back = (
            jnp.einsum("hsk,khd->shd", score_back, key_blk, preferred_element_type=jnp.float32)
            * head_scale
        )
        key_back = (
            jnp.einsum("hsk,shd->khd", score_back, query_blk, preferred_element_type=jnp.float32)
            * head_scale
        )
        return (query_back, key_back, value_back)

    query_back, key_back, value_back = lax.map(
        attend_back,
        (
            query_cls,
            key_rows.reshape(block_shape),
            value_rows.reshape(block_shape),
            mixed_cls,
            log_cls,
            buckets,
            lengths,
            slot_starts,
        ),
    )
    query_back = query_back.reshape(cls_count, width).astype(jnp.bfloat16)
    key_back = key_back.reshape(tok_rows, width).astype(jnp.bfloat16)
    value_back = value_back.reshape(tok_rows, width).astype(jnp.bfloat16)
    b_query_grad = jnp.sum(query_back.astype(jnp.float32), axis=0)
    w_query_grad = matmul_tn(tokens[cand_rows], query_back)
    w_key_grad = matmul_tn(tokens, key_back)
    w_value_grad = matmul_tn(tokens, value_back)
    b_value_grad = jnp.sum(value_back.astype(jnp.float32), axis=0)
    row_grad = one_grad + matmul_nt(query_back, w_query)
    tokens_grad = (
        (matmul_nt(key_back, w_key) + matmul_nt(value_back, w_value)).at[cand_rows].add(row_grad)
    )
    all_shares = (
        lax.psum_scatter(w_query_grad, "batch", scatter_dimension=0, tiled=True),
        lax.psum_scatter(b_query_grad, "batch", scatter_dimension=0, tiled=True),
        lax.psum_scatter(w_key_grad, "batch", scatter_dimension=0, tiled=True),
        lax.psum_scatter(w_value_grad, "batch", scatter_dimension=0, tiled=True),
        lax.psum_scatter(b_value_grad, "batch", scatter_dimension=0, tiled=True),
        lax.psum_scatter(w_out_grad, "batch", scatter_dimension=0, tiled=True),
        lax.psum_scatter(b_out_grad, "batch", scatter_dimension=0, tiled=True),
        lax.psum_scatter(gain_attn_grad, "batch", scatter_dimension=0, tiled=True),
        lax.psum_scatter(shift_attn_grad, "batch", scatter_dimension=0, tiled=True),
        lax.psum_scatter(w_in_grad, "batch", scatter_dimension=0, tiled=True),
        lax.psum_scatter(b_in_grad, "batch", scatter_dimension=0, tiled=True),
        lax.psum_scatter(w_back_grad, "batch", scatter_dimension=0, tiled=True),
        lax.psum_scatter(b_back_grad, "batch", scatter_dimension=0, tiled=True),
        lax.psum_scatter(gain_ffn_grad, "batch", scatter_dimension=0, tiled=True),
        lax.psum_scatter(shift_ffn_grad, "batch", scatter_dimension=0, tiled=True),
    )
    summed = tuple(
        lax.psum(
            (
                all_shares[0],
                all_shares[1],
                all_shares[2],
                all_shares[3],
                all_shares[4],
                all_shares[5],
                all_shares[6],
                all_shares[7],
                all_shares[8],
                all_shares[9],
                all_shares[10],
                all_shares[11],
                all_shares[12],
                all_shares[13],
                all_shares[14],
            ),
            "grp",
        )
    )
    return (
        encoded,
        tokens_grad,
        summed[0],
        summed[1],
        summed[2],
        summed[3],
        summed[4],
        summed[5],
        summed[6],
        summed[7],
        summed[8],
        summed[9],
        summed[10],
        summed[11],
        summed[12],
        summed[13],
        summed[14],
    )


def solution(mesh):
    in_specs = (
        P(("grp", "batch"), None),
        P(("grp", "batch")),
        P(("grp", "batch"), None),
        P(),
        P(),
        P(),
        P(),
        P(),
        P(),
        P(),
        P(),
        P(),
        P(),
        P(),
        P(),
        P(),
        P(),
        P(),
        P(),
    )
    out_specs = (
        P(("grp", "batch"), None),
        P(("grp", "batch"), None),
        P("batch", None),
        P("batch"),
        P("batch", None),
        P("batch", None),
        P("batch"),
        P("batch", None),
        P("batch"),
        P("batch"),
        P("batch"),
        P("batch", None),
        P("batch"),
        P("batch", None),
        P("batch"),
        P("batch"),
        P("batch"),
    )
    return jax.shard_map(shards, mesh=mesh, in_specs=in_specs, out_specs=out_specs, check_vma=False)
```

profile of v0, /device:TPU:0, one launch (start us, length us, event | category | flops | bytes accessed | tf_op | source)
XLA Modules:
  0.0 929.9 jit_solution(15561824877209814522)
XLA Ops:
  13.5 2.6 copy.102
  16.2 3.8 add_convert_fusion
  20.0 2.6 copy.104
  22.5 2.9 reshape.467
  27.7 2.5 add_convert_fusion.1
  32.0 2.4 reshape.466
  34.4 3.1 copy.106
  37.5 2.5 convolution_convert_fusion
  41.7 2.4 reshape.468
  45.8 30.7 %while.30 = (s32[]{:T(128)}, bf16[2,512,12,64]{1,3,2,0:T(8,128)(2,1)}, f32[2,12,512]{2,1,0:T(8,128)S(1)}, bf16[2,512,12,64]{1,3,2,0:T(8,128)(2,1)}, s32[2]{0:T(1...) while((s32[]{:T(128)}, ...), condition=%wide.region_4.5_spmd, body=%wide.region_0.4_spmd.sunk | while | flops 844000256 | bytes 42177956 | solution.py:130
  50.1 3.2 fusion.156
  53.3 2.6 fusion.157
  55.9 5.5 fusion.158
  65.3 3.2 fusion.156
  68.5 2.6 fusion.157
  71.0 5.5 fusion.158
  76.6 3.6 copy.109
  84.1 36.7 %fusion.52 = (bf16[1024,3072]{1,0:T(8,128)(2,1)S(1)}, f32[1024,3072]{1,0:T(8,128)}) fusion(f32[3072]{0:T(1024)S(1)} %copy-done.58, bf16[1024,768]{0,1:T(8,128)(2,1)S(1)} %fusion.60, bf16[768,3072]{1,0:T(8,128)(2,1)S(1)} %bitcast.204), kind=kOutput, calls=%fused_computation.96 | convolution fusion | flops 5039456256 | bytes 25178112 | tf_op jit(solution)/shard_map/dot_general | solution.py:20
  120.8 9.4 %fusion.90 = (f32[1024]{0:T(1024)S(1)}, f32[1024,768]{0,1:T(8,128)S(1)}) fusion(f32[768]{0:T(1024)S(1)} %copy-done.62, bf16[1024,3072]{1,0:T(8,128)(2,1)S(1)} %get-tuple-element.518, bf16[3072,768]{1,0:T(8,128)(2,1)} %param.38, f32[768]{0:T(1024)S(1)} %copy-done.46, f32[768]{0:T(1024)S(1)} %copy-done.36, f32[1024]{0:T(1024)S(1)} %add_rsqrt_fusion.1, ...), kind=kOutput, calls=%fused_computation.222 | convolution fusion | flops 4837342208 | bytes 17323008 | tf_op jit(solution)/shard_map/dot_general | solution.py:20
  134.2 3.0 gather_fusion.3
  137.5 3.5 copy.112
  141.1 3.6 copy.111
  146.5 2.3 gather_fusion.1
  148.9 4.2 gather_fusion.12
  153.2 2.6 gather_fusion.7
  155.8 5.4 gather_fusion.6
  161.2 2.5 gather_fusion.5
  165.2 30.3 %all-gather.2.cloned.1.call-done = bf16[1024,768]{1,0:T(8,128)(2,1)} async-done(((bf16[32,768]{1,0:T(8,128)(2,1)}), bf16[1024,768]{1,0:T(8,128)(2,1)}) %all-gather.2.cloned.1.call-update) | async-done | bytes 1572880 | tf_op jit(solution)/shard_map/all_gather | solution.py:159
  198.6 73.2 %fusion = f32[8,768]{1,0:T(8,128)S(1)} fusion(f32[192,768]{1,0:T(8,128)S(1)} %concatenate.3), kind=kCustom, calls=%all-reduce-scatter | all-reduce-scatter fusion | flops 196609 | bytes 614400
  274.4 2.2 collective-permute-start.7
  278.1 6.6 collective-permute-start.3
  284.8 2.2 collective-permute-start.2
  287.0 4.0 collective-permute-start.1
  292.3 5.2 all_gather.7
  299.9 4.7 convert_reduce_fusion.1
  304.6 4.6 multiply_reduce_fusion.4
  310.9 19.4 %while.31 = (s32[]{:T(128)}, bf16[2,16,12,64]{3,1,2,0:T(8,128)(2,1)}, bf16[2,512,12,64]{1,3,2,0:T(8,128)(2,1)}, bf16[2,512,12,64]{1,3,2,0:T(8,128)(2,1)}, bf16[2...) while((s32[]{:T(128)}, ...), condition=%wide.region_25.26_spmd, body=%wide.region_22.25_spmd.sunk | while | flops 64763768 | bytes 34578836 | solution.py:240
  330.3 3.1 copy.118
  335.1 2.8 convolution_bitcast_fusion
  337.9 3.1 copy.128
  341.0 3.0 copy.117
  345.6 2.8 convolution_bitcast_fusion.1
  348.4 3.4 copy.126
  351.9 2.4 gather_fusion.8
  354.5 1.9 fusion.93
  358.1 2.4 gather_fusion.9
  360.5 2.0 fusion.94
  364.1 2.3 gather_fusion.10
  366.4 5.0 fusion.95
  371.5 4.5 gather_fusion.11
  376.0 5.1 fusion.96
  381.1 20.2 %reduce-scatter.23.cloned.1.call-done = f32[48,768]{1,0:T(8,128)} async-done(((f32[768,768]{1,0:T(8,128)}), f32[48,768]{1,0:T(8,128)}) %reduce-scatter.23.cloned.1.call-update) | async-done | bytes 147472
  401.3 1.8 copy.129
  403.1 64.5 %reduce-scatter.21.cloned.1.call-done = f32[48,768]{1,0:T(8,128)} async-done(((f32[768,768]{1,0:T(8,128)}), f32[48,768]{1,0:T(8,128)}) %reduce-scatter.21.cloned.1.call-update) | async-done | bytes 147472
  469.4 64.4 %reduce-scatter.13.cloned.1.call-done = f32[48,768]{1,0:T(8,128)} async-done(((f32[768,768]{1,0:T(8,128)}), f32[48,768]{1,0:T(8,128)}) %reduce-scatter.13.cloned.1.call-update) | async-done | bytes 147472 | tf_op jit(solution)/shard_map/reduce_scatter | solution.py:266
  533.8 66.1 %reduce-scatter.15.cloned.1.call-done = f32[48,768]{1,0:T(8,128)} async-done(((f32[768,768]{1,0:T(8,128)}), f32[48,768]{1,0:T(8,128)}) %reduce-scatter.15.cloned.1.call-update) | async-done | bytes 147472 | tf_op jit(solution)/shard_map/reduce_scatter | solution.py:271
  599.9 114.3 %reduce-scatter.17.cloned.1.call-done = f32[48,3072]{1,0:T(8,128)} async-done(((f32[768,3072]{1,0:T(8,128)}), f32[48,3072]{1,0:T(8,128)}) %reduce-scatter.17.cloned.1.call-update) | async-done | bytes 589840 | tf_op jit(solution)/shard_map/reduce_scatter | solution.py:275
  714.2 115.8 %reduce-scatter.19.cloned.1.call-done = f32[192,768]{1,0:T(8,128)} async-done(((f32[3072,768]{1,0:T(8,128)}), f32[192,768]{1,0:T(8,128)}) %reduce-scatter.19.cloned.1.call-update) | async-done | bytes 589840 | tf_op jit(solution)/shard_map/reduce_scatter | solution.py:277
  835.4 60.4 %all-reduce.13 = (f32[768]{0:T(1024)S(1)}, f32[768]{0:T(1024)S(1)}, f32[768]{0:T(1024)S(1)}, f32[768]{0:T(1024)S(1)}, f32[768]{0:T(1024)S(1)}, /*index=5*/f32[30...) all-reduce(f32[768]{0:T(1024)S(1)} %reduce_sum.296, ...), channel_id=4, replica_groups=mesh['grp'=2,'batch'=16] {'batch'}, use_global_device_ids=true, to_apply=%region_30.31.clone | all-reduce | flops 9216 | bytes 73728
  900.0 3.2 convolution_add_fusion
  903.2 4.3 scatter_fusion
  907.5 5.5 all-reduce.14
  913.0 1.9 copy.123
  919.9 1.9 copy.170
  (340 shorter events, 81.8 us)
Async XLA Ops:
  7.2 30.3 %copy-start = (bf16[768,768]{1,0:T(8,128)(2,1)S(1)}, bf16[768,768]{1,0:T(8,128)(2,1)}, u32[]{:S(2)}) copy-start(bf16[768,768]{1,0:T(8,128)(2,1)} %param.29) | copy-start | bytes 3538948
  7.2 8.9 copy-start.13
  7.2 8.9 copy-start.59
  7.2 188.3 %all-gather.2.cloned.1.call-start = ((), (), s32[]{:S(2)}) async-start(), calls=%async_computation.6 | async-start | bytes 1622016 | tf_op jit(solution)/shard_map/all_gather | solution.py:159
  8.1 3.6 copy-start.54
  22.5 4.4 copy-start.60
  25.4 2.3 copy-start.56
  34.4 3.1 copy-start.15
  76.5 4.1 copy-start.1
  76.5 4.1 copy-start.23
  76.6 4.1 copy-start.24
  76.6 4.1 copy-start.61
  76.6 7.5 slice-start
  80.7 3.4 slice-start.1
  82.4 38.4 %copy-start.3 = (f32[1024,768]{0,1:T(8,128)}, f32[1024,768]{0,1:T(8,128)S(1)}, u32[]{:S(2)}) copy-start(f32[1024,768]{0,1:T(8,128)S(1)} %get-tuple-element.517) | copy-start | bytes 9437188
  84.1 36.7 %copy-start.11 = (bf16[1024,768]{0,1:T(8,128)(2,1)}, bf16[1024,768]{0,1:T(8,128)(2,1)S(1)}, u32[]{:S(2)}) copy-start(bf16[1024,768]{0,1:T(8,128)(2,1)S(1)} %fusion.60) | copy-start | bytes 4718596
  84.1 36.7 %copy-start.62 = (f32[768]{0:T(1024)S(1)}, f32[768]{0:T(1024)}, u32[]{:S(2)}) copy-start(f32[768]{0:T(1024)} %param.39) | copy-start | bytes 9220
  120.8 9.4 %copy-start.32 = (bf16[1024,3072]{1,0:T(8,128)(2,1)}, bf16[1024,3072]{1,0:T(8,128)(2,1)S(1)}, u32[]{:S(2)}) copy-start(bf16[1024,3072]{1,0:T(8,128)(2,1)S(1)} %get-tuple-element.518) | copy-start | bytes 18874372
  131.9 5.4 copy-start.64
  131.9 5.5 copy-start.53
  132.4 8.6 copy-start.5
  137.3 264.0 %reduce-scatter.23.cloned.1.call-start = ((), (), s32[]{:S(2)}) async-start(), calls=%async_computation.12 | async-start | bytes 2506752
  141.0 3.6 copy-start.67
  141.0 5.2 copy-start.55
  141.0 5.3 copy-start.43
  141.1 5.3 copy-start.45
  146.4 6.7 copy-start.50
  146.5 14.8 %copy-start.40 = (s32[1024]{0:T(1024)}, s32[1024]{0:T(1024)S(1)}, u32[]{:S(2)}) copy-start(s32[1024]{0:T(1024)S(1)} %pad_clamp_fusion.4) | copy-start | bytes 12292
  271.8 15.2 %collective-permute-start.6 = (f32[8,768]{1,0:T(8,128)S(1)}, f32[8,768]{1,0:T(8,128)S(1)}, u32[]{:S(2)}, u32[]{:S(2)}) collective-permute-start(f32[8,768]{1,0:T(8,128)S(1)} %fusion), channel_id=1, source_target_pairs={{0,7},{1,8},{2,9},{3,10},{4,11},{5,12},{6,13},{7,14},{8,15},{9,16}... | collective-permute-start | bytes 73736
  273.1 17.9 %collective-permute-start.5 = (f32[8,768]{1,0:T(8,128)S(1)}, f32[8,768]{1,0:T(8,128)S(1)}, u32[]{:S(2)}, u32[]{:S(2)}) collective-permute-start(f32[8,768]{1,0:T(8,128)S(1)} %fusion), channel_id=1, source_target_pairs={{0,6},{1,7},{2,8},{3,9},{4,10},{5,11},{6,12},{7,13},{8,14},{9,15},... | collective-permute-start | bytes 73736
  274.4 10.4 %collective-permute-start.7 = (f32[6,768]{1,0:T(8,128)S(1)}, f32[6,768]{1,0:T(8,128)S(1)}, u32[]{:S(2)}, u32[]{:S(2)}) collective-permute-start(f32[6,768]{1,0:T(8,128)S(1)} %slice.38), channel_id=1, source_target_pairs={{0,8},{1,9},{2,10},{3,11},{4,12},{5,13},{6,14},{7,15},{8,16},{9,17... | collective-permute-start | bytes 55304
  276.8 20.7 %collective-permute-start.4 = (f32[8,768]{1,0:T(8,128)S(1)}, f32[8,768]{1,0:T(8,128)S(1)}, u32[]{:S(2)}, u32[]{:S(2)}) collective-permute-start(f32[8,768]{1,0:T(8,128)S(1)} %fusion), channel_id=1, source_target_pairs={{0,5},{1,6},{2,7},{3,8},{4,9},{5,10},{6,11},{7,12},{8,13},{9,14},{... | collective-permute-start | bytes 73736
  278.1 19.4 %collective-permute-start.3 = (f32[8,768]{1,0:T(8,128)S(1)}, f32[8,768]{1,0:T(8,128)S(1)}, u32[]{:S(2)}, u32[]{:S(2)}) collective-permute-start(f32[8,768]{1,0:T(8,128)S(1)} %fusion), channel_id=1, source_target_pairs={{0,4},{1,5},{2,6},{3,7},{4,8},{5,9},{6,10},{7,11},{8,12},{9,13},{1... | collective-permute-start | bytes 73736
  284.8 12.8 %collective-permute-start.2 = (f32[8,768]{1,0:T(8,128)S(1)}, f32[8,768]{1,0:T(8,128)S(1)}, u32[]{:S(2)}, u32[]{:S(2)}) collective-permute-start(f32[8,768]{1,0:T(8,128)S(1)} %fusion), channel_id=1, source_target_pairs={{0,3},{1,4},{2,5},{3,6},{4,7},{5,8},{6,9},{7,10},{8,11},{9,12},{10... | collective-permute-start | bytes 73736
  287.0 10.6 %collective-permute-start.1 = (f32[8,768]{1,0:T(8,128)S(1)}, f32[8,768]{1,0:T(8,128)S(1)}, u32[]{:S(2)}, u32[]{:S(2)}) collective-permute-start(f32[8,768]{1,0:T(8,128)S(1)} %fusion), channel_id=1, source_target_pairs={{0,2},{1,3},{2,4},{3,5},{4,6},{5,7},{6,8},{7,9},{8,10},{9,11},{10,... | collective-permute-start | bytes 73736
  291.0 6.6 collective-permute-start
  299.9 4.7 copy-start.33
  304.6 5.5 copy-start.25
  304.6 6.3 copy-start.2
  317.2 3.4 copy-start.44
  326.9 3.4 copy-start.44
  330.3 4.8 copy-start.16
  341.0 126.6 %reduce-scatter.21.cloned.1.call-start = ((), (), s32[]{:S(2)}) async-start(), calls=%async_computation.11 | async-start | bytes 2506752
  348.4 3.5 copy-start.41
  348.4 5.9 copy-start.31
  351.8 4.6 copy-start.8
  351.8 182.0 %reduce-scatter.13.cloned.1.call-start = ((), (), s32[]{:S(2)}) async-start(), calls=%async_computation.7 | async-start | bytes 2506752 | tf_op jit(solution)/shard_map/reduce_scatter | solution.py:266
  356.4 4.1 copy-start.28
  356.4 243.5 %reduce-scatter.15.cloned.1.call-start = ((), (), s32[]{:S(2)}) async-start(), calls=%async_computation.8 | async-start | bytes 2506752 | tf_op jit(solution)/shard_map/reduce_scatter | solution.py:271
  358.1 4.5 copy-start.12
  362.5 351.8 %reduce-scatter.17.cloned.1.call-start = ((), (), s32[]{:S(2)}) async-start(), calls=%async_computation.9 | async-start | bytes 10027008 | tf_op jit(solution)/shard_map/reduce_scatter | solution.py:275
  371.4 4.6 copy-start.34
  371.4 458.6 %reduce-scatter.19.cloned.1.call-start = ((), (), s32[]{:S(2)}) async-start(), calls=%async_computation.10 | async-start | bytes 10027008 | tf_op jit(solution)/shard_map/reduce_scatter | solution.py:277
  381.1 449.0 %copy-start.6 = (bf16[1024,768]{0,1:T(8,128)(2,1)S(1)}, bf16[1024,768]{0,1:T(8,128)(2,1)}, u32[]{:S(2)}) copy-start(bf16[1024,768]{0,1:T(8,128)(2,1)} %copy-done.5) | copy-start | bytes 4718596
  381.1 450.6 %copy-start.65 = (u32[32]{0:T(128)S(1)}, u32[32]{0:T(128)}, u32[]{:S(2)}) copy-start(u32[32]{0:T(128)} %constant.355) | copy-start | bytes 388
  381.1 531.9 %all-reduce.18.cloned.1.call-start = ((), (), s32[]{:S(2)}) async-start(), calls=%async_computation.13 | async-start | bytes 4521984 | tf_op jit(solution)/shard_map/psum | solution.py:283
  830.0 5.4 copy-start.37
  830.0 5.4 copy-start.38
  830.0 5.4 copy-start.39
  830.0 5.4 copy-start.42
  830.0 66.4 %copy-start.49 = (f32[32]{0:T(128)S(1)}, f32[32]{0:T(128)}, u32[]{:S(2)}) copy-start(f32[32]{0:T(128)} %copy-done.48) | copy-start | bytes 388
  831.7 66.5 %copy-start.22 = (bf16[96,8,2,512]{3,1,2,0:T(8,128)(2,1)S(1)}, bf16[96,8,2,512]{3,1,2,0:T(8,128)(2,1)}, u32[]{:S(2)}) copy-start(bf16[96,8,2,512]{3,1,2,0:T(8,128)(2,1)} %copy-done.21) | copy-start | bytes 4718596
  900.0 3.2 copy-start.51
  913.0 8.7 copy-start.26
  (29 other events, 39.4 us)
Sparse Core Ops, SparseCore 0:
  137.4 58.1 all-gather.1
  341.1 60.1 reduce-scatter.22
  405.5 62.0 reduce-scatter.20
  471.8 61.9 reduce-scatter.12
  537.9 61.9 reduce-scatter.14
  603.9 110.3 reduce-scatter.16
  718.9 111.1 reduce-scatter.18
  833.3 67.1 all-reduce.17
where the time goes:
time: 937 us; the launch traced here: 930 us
  waiting for transfers between devices  476 us (51%)
  blocking collectives  144 us (15%)
  local copies, waits for them, and re-layouts  127 us (14%)
  matrix products  116 us (12%)
  other arithmetic  23.2 us (2%)
  starting transfers between devices  20.6 us (2%)
  between operations  17 us (2%)
    unnamed x2, blocking collectives  134 us
    reduce_scatter x1, waiting for transfers between devices, shards(): lax.psum_scatter(w_back_grad, 'batch', scatter_dimension=0, tiled=True)  116 us
    reduce_scatter x1, waiting for transfers between devices, shards(): lax.psum_scatter(w_in_grad, 'batch', scatter_dimension=0, tiled=True)  114 us
    unnamed x18, waiting for transfers between devices  84.8 us
    reduce_scatter x1, waiting for transfers between devices, shards(): lax.psum_scatter(w_out_grad, 'batch', scatter_dimension=0, tiled=True)  66.1 us
    reduce_scatter x1, waiting for transfers between devices, shards(): lax.psum_scatter(w_query_grad, 'batch', scatter_dimension=0, tiled=True)  64.4 us
    dot_general x7, matrix products, matmul(): return jnp.dot(left, right, preferred_element_type=jnp.float32)  56.8 us
    unnamed x154, local copies, waits for them, and re-layouts  34.8 us
  transfers between devices with their start and end apart: 16, of which 7 were waited for; matrix products, arithmetic and copies ran while one was open for 9% of the time, Pallas kernels for 0%

commit v1 on v0

--- a/solution.py
+++ b/solution.py
@@ -1,6 +1,11 @@
+import functools
+import typing
+
 import jax
 import jax.numpy as jnp
 from jax import lax
+from jax.experimental import pallas as pl
+from jax.experimental.pallas import tpu as pltpu
 from jax.sharding import PartitionSpec as P
 
 H = 12
@@ -80,7 +85,7 @@
     return (jax.nn.softmax(scores, axis=1) - targets).astype(jnp.bfloat16)
 
 
-def shards(
+def plain_shards(
     tokens,
     buckets,
     lengths,
@@ -322,6 +327,1196 @@
     )
 
 
+MESH = pl.DeviceIdType.MESH
+HEADS_VREG = 4
+PART = 16
+
+
+def nn(left, right):
+    return lax.dot_general(
+        left, right, (((1,), (0,)), ((), ())), preferred_element_type=jnp.float32
+    )
+
+
+def nt(left, right):
+    return lax.dot_general(
+        left, right, (((1,), (1,)), ((), ())), preferred_element_type=jnp.float32
+    )
+
+
+def tn(left, right):
+    return lax.dot_general(
+        left, right, (((0,), (0,)), ((), ())), preferred_element_type=jnp.float32
+    )
+
+
+def low(values):
+    return values.astype(jnp.bfloat16)
+
+
+def wide(values):
+    return values.astype(jnp.float32)
+
+
+def iota(shape, axis):
+    return lax.broadcasted_iota(jnp.int32, shape, axis)
+
+
+def gelu(values):
+    middle = 0.5 * values
+    return middle + middle * lax.erf(values * 0.7071067811865476)
+
+
+def gelu_slope(values):
+    below = 0.5 + 0.5 * lax.erf(values * 0.7071067811865476)
+    return below + values * (0.3989422804014327 * jnp.exp(-0.5 * (values * values)))
+
+
+def gelu_both(values):
+    below = 0.5 + 0.5 * lax.erf(values * 0.7071067811865476)
+    bell = 0.3989422804014327 * jnp.exp(-0.5 * (values * values))
+    return values * below, below + values * bell
+
+
+def unit_rows(hidden):
+    center = hidden - jnp.mean(hidden, axis=-1, keepdims=True)
+    rate = lax.rsqrt(jnp.mean(center * center, axis=-1, keepdims=True) + norm_epsilon)
+    return center * rate, rate
+
+
+def norm_back(grad, unit, rate, gain):
+    scaled = grad * gain
+    return rate * (
+        scaled
+        - jnp.mean(scaled, axis=-1, keepdims=True)
+        - unit * jnp.mean(scaled * unit, axis=-1, keepdims=True)
+    )
+
+
+def hold(sem, ref):
+    pltpu.make_async_copy(ref, ref, sem).wait()
+
+
+def pack_eight(values):
+    middle = values.shape[1] // 2
+    values = wide(values)
+    return low(jnp.concatenate([values[:, :middle], values[:, middle:]], axis=0))
+
+
+def unpack_eight(values):
+    count, _, middle = values.shape
+    values = wide(values)
+    return jnp.concatenate(
+        [values[:, 0:8].reshape(8 * count, middle), values[:, 8:16].reshape(8 * count, middle)], axis=1
+    )
+
+
+class Ins(typing.NamedTuple):
+    tokens: typing.Any
+    buckets: typing.Any
+    lengths: typing.Any
+    positives: typing.Any
+    w_query: typing.Any
+    b_query: typing.Any
+    w_key: typing.Any
+    w_value: typing.Any
+    b_value: typing.Any
+    w_out: typing.Any
+    b_out: typing.Any
+    gain_attn: typing.Any
+    shift_attn: typing.Any
+    w_in: typing.Any
+    b_in: typing.Any
+    w_back: typing.Any
+    b_back: typing.Any
+    gain_ffn: typing.Any
+    shift_ffn: typing.Any
+
+
+class Outs(typing.NamedTuple):
+    encoded: typing.Any
+    left_out: typing.Any
+    right_out: typing.Any
+    g_query: typing.Any
+    gb_query: typing.Any
+    g_key: typing.Any
+    g_value: typing.Any
+    gb_value: typing.Any
+    g_out: typing.Any
+    gb_out: typing.Any
+    g_gain_attn: typing.Any
+    g_shift_attn: typing.Any
+    g_in: typing.Any
+    gb_in: typing.Any
+    g_back: typing.Any
+    gb_back: typing.Any
+    g_gain_ffn: typing.Any
+    g_shift_ffn: typing.Any
+
+
+class Scratch(typing.NamedTuple):
+    tokens_v: typing.Any
+    w_query_v: typing.Any
+    w_key_v: typing.Any
+    w_value_v: typing.Any
+    w_out_v: typing.Any
+    w_in_v: typing.Any
+    w_back_v: typing.Any
+    vectors_v: typing.Any
+    b_in_1d: typing.Any
+    vector_sem: typing.Any
+    rows_v: typing.Any
+    t_sum: typing.Any
+    b_in_v: typing.Any
+    key_seg: typing.Any
+    left: typing.Any
+    right: typing.Any
+    prob: typing.Any
+    slope: typing.Any
+    unit_one: typing.Any
+    rate_one: typing.Any
+    unit_two: typing.Any
+    rate_two: typing.Any
+    cls: typing.Any
+    y_grad: typing.Any
+    x_all: typing.Any
+    mixed_all: typing.Any
+    normed_all: typing.Any
+    branch_all: typing.Any
+    attn_all: typing.Any
+    query_all: typing.Any
+    few_all: typing.Any
+    few_out: typing.Any
+    t_side: typing.Any
+    u_side: typing.Any
+    u_twin: typing.Any
+    t_few: typing.Any
+    u_few: typing.Any
+    side_got: typing.Any
+    few_got: typing.Any
+    sum_out: typing.Any
+    sum_in: typing.Any
+    pas_out: typing.Any
+    pas_in: typing.Any
+    pas_part: typing.Any
+    pas_twin: typing.Any
+    pas_sum: typing.Any
+    pas_got: typing.Any
+    normed_v: typing.Any
+    enc_v: typing.Any
+    flat_a: typing.Any
+    flat_b: typing.Any
+    flat_c: typing.Any
+    flat_d: typing.Any
+    factor: typing.Any
+    stage: typing.Any
+    swap_out0: typing.Any
+    swap_in0: typing.Any
+    swap_out1: typing.Any
+    swap_in1: typing.Any
+    load_sem: typing.Any
+    store_sem: typing.Any
+    g_send: typing.Any
+    g_recv: typing.Any
+    f_send: typing.Any
+    f_recv: typing.Any
+    v_send: typing.Any
+    v_recv: typing.Any
+    a_send: typing.Any
+    a_recv: typing.Any
+    b_send: typing.Any
+    b_recv: typing.Any
+    s_send: typing.Any
+    s_recv: typing.Any
+
+
+class Refs:
+    pass
+
+
+X_ALL, MIXED_ALL, NORMED_ALL, BRANCH_ALL, ATTN_ALL, QUERY_ALL, FEW_ALL, LAST_ALL = range(8)
+TO_QUERY = (X_ALL, NORMED_ALL, BRANCH_ALL, QUERY_ALL)
+TO_PASSAGE = (MIXED_ALL, NORMED_ALL, BRANCH_ALL, ATTN_ALL)
+EARLY, LATE = range(2)
+B_QUERY, B_VALUE, B_OUT, GAIN_ATTN, SHIFT_ATTN, B_BACK, GAIN_FFN, SHIFT_FFN = range(8)
+W_QUERY, W_KEY, W_VALUE, W_OUT, W_IN, W_BACK, TOKENS = range(7)
+
+
+def main_kernel(sizes, *refs):
+    groups, members, rows, width, hidden = sizes
+    r = Refs()
+    ends = (len(Ins._fields), len(Ins._fields) + len(Outs._fields))
+    for group in (Ins(*refs[: ends[0]]), Outs(*refs[ends[0] : ends[1]]), Scratch(*refs[ends[1] :])):
+        r.__dict__.update(group._asdict())
+    across = members // 8
+    depth = 4
+    share = width // members
+    cand = rows // QLEN
+    lanes = H * cand
+    slots = members
+    query_rows = slots * cand
+    all_rows = query_rows + slots * 8
+    half = width // 2
+    score_scale = width ** (-0.5)
+
+    grp = lax.axis_index("grp")
+    bat = lax.axis_index("batch")
+    core = lax.rem(bat, 2)
+    col = lax.rem(lax.div(bat, 2), across)
+    lay = lax.div(bat, 2 * across)
+    sibling = bat + 1 - 2 * core
+    is_query = grp == 0
+    is_passage = grp > 0
+
+    def slot_of(member):
+        return (
+            lax.rem(member, 2) * across + lax.rem(lax.div(member, 2), across)
+        ) * depth + lax.div(member, 2 * across)
+
+    my_slot = slot_of(bat)
+
+    weights = (r.w_query, r.w_key, r.w_value, r.w_out, r.w_in, r.w_back, r.tokens)
+    held = (r.w_query_v, r.w_key_v, r.w_value_v, r.w_out_v, r.w_in_v, r.w_back_v, r.tokens_v)
+
+    def load(at):
+        return pltpu.make_async_copy(weights[at], held[at], r.load_sem.at[at])
+
+    load(TOKENS).start()
+
+    vectors = (
+        r.b_query,
+        r.b_value,
+        r.b_out,
+        r.gain_attn,
+        r.shift_attn,
+        r.b_back,
+        r.gain_ffn,
+        r.shift_ffn,
+    )
+    vector_loads = [
+        pltpu.make_async_copy(vector, r.vectors_v.at[at], r.vector_sem.at[at]) for at, vector in enumerate(vectors)
+    ]
+    vector_loads.append(pltpu.make_async_copy(r.b_in, r.b_in_1d, r.vector_sem.at[len(vectors)]))
+    for copy in vector_loads:
+        copy.start()
+    for at in (W_QUERY, W_KEY):
+        load(at).start()
+
+    barrier = pltpu.get_barrier_semaphore()
+
+    def greet(step, carry):
+        other = lax.rem(bat + step, members)
+
+        @pl.when(step > 0)
+        def _():
+            pl.semaphore_signal(barrier, inc=1, device_id=(grp, other), device_id_type=MESH)
+
+        pl.semaphore_signal(barrier, inc=1, device_id=(1 - grp, other), device_id_type=MESH)
+        return carry
+
+    lax.fori_loop(0, members, greet, 0)
+
+    def remote(src, dst, send, recv, to):
+        return pltpu.make_async_remote_copy(
+            src_ref=src, dst_ref=dst, send_sem=send, recv_sem=recv, device_id=to, device_id_type=MESH
+        )
+
+    def vec(at):
+        return r.rows_v[at : at + 1, :]
+
+    def bucket_of(block):
+        return r.buckets[block]
+
+    def size_of(bucket):
+        return jnp.where(bucket == 0, QLEN, jnp.where(bucket == 1, SHORT, LONG))
+
+    def count_of(bucket):
+        return jnp.where(bucket == 0, BLK // QLEN, jnp.where(bucket == 1, BLK // SHORT, BLK // LONG))
+
+    first, second = bucket_of(0), bucket_of(1)
+    first_count, second_count = count_of(first), count_of(second)
+
+    def listed(index):
+        later = index - first_count
+        inside = index < first_count + second_count
+        place = jnp.where(index < first_count, index * size_of(first), BLK + later * size_of(second))
+        segment = jnp.where(index < first_count, index, SLOTS_BLK + later)
+        return jnp.where(inside, place, -1), jnp.where(inside, segment, -2)
+
+    def segment_of(token, bucket):
+        within = token & (BLK - 1)
+        slot = jnp.where(
+            bucket == 0, within >> 5, jnp.where(bucket == 1, within >> 7, within >> 8)
+        )
+        place = jnp.where(
+            bucket == 0, within & (QLEN - 1), jnp.where(bucket == 1, within & (SHORT - 1), within & (LONG - 1))
+        )
+        return slot + SLOTS_BLK * (token >> 9), place
+
+    token = iota((1, rows), 1)
+    bucket_row = jnp.where(token < BLK, first, second)
+    segment_row, place_row = segment_of(token, bucket_row)
+    limit_row = jnp.zeros((1, rows), jnp.int32)
+    for at in range(rows // BLK * SLOTS_BLK):
+        used = r.lengths[at // SLOTS_BLK, at % SLOTS_BLK]
+        limit_row = jnp.where(segment_row == at, used, limit_row)
+    key_segment = jnp.where(place_row < limit_row, segment_row, -1)
+    for at in range(rows // 256):
+        r.key_seg[at] = key_segment[:, 256 * at : 256 * at + 256]
+
+    lane_head = iota((cand, width), 1) >> 6
+
+    def by_head(values):
+        values = wide(values)
+        return low(
+            jnp.concatenate([jnp.where(lane_head == h, values, 0.0) for h in range(H)], axis=0)
+        )
+
+    def pick_heads(values):
+        total = jnp.zeros((cand, width), jnp.float32)
+        for h in range(H):
+            total = total + jnp.where(lane_head == h, values[h * cand : (h + 1) * cand], 0.0)
+        return total
+
+    gathered = (r.x_all, r.mixed_all, r.normed_all, r.branch_all, r.attn_all, r.query_all, r.few_all.at[EARLY], r.few_all.at[LATE])
+
+    def keep(name, values):
+        @pl.when(is_query)
+        def _():
+            gathered[name][core, col, lay, 0:cand] = values[:, :half]
+            gathered[name][core, col, lay, cand : 2 * cand] = values[:, half:]
+
+        @pl.when(is_passage)
+        def _():
+            packed = pack_eight(values[0:8])
+            if name in TO_QUERY:
+                when, at = divmod(TO_QUERY.index(name), 2)
+                r.few_out[when, PART * at : PART * at + PART] = packed
+            if name in TO_PASSAGE:
+                when, at = divmod(TO_PASSAGE.index(name), 2)
+                r.few_all[when, core, col, lay, PART * at : PART * at + PART] = packed
+
+    def few_rows(values):
+        eight = values.reshape(H, cand, width)[:, 0:8].reshape(8 * H, width)
+        return low(jnp.concatenate([eight, jnp.zeros((128 - 8 * H, width), jnp.float32)], axis=0).T)
+
+    def goes_to(name):
+        if name == FEW_ALL or name in TO_QUERY and name in TO_PASSAGE:
+            return grp >= 0
+        return is_query if name in TO_QUERY else is_passage
+
+    def sems(name, stage):
+        return r.g_send.at[name, stage], r.g_recv.at[name, stage]
+
+    def my_piece(name):
+        return gathered[name].at[core, col, lay]
+
+    def go(name, stage):
+        buf = gathered[name]
+        send, recv = sems(name, stage)
+        if stage == 0:
+
+            @pl.when(is_passage if name == FEW_ALL else is_query)
+            def _():
+                src = r.few_out.at[EARLY] if name == FEW_ALL else my_piece(name)
+                remote(src, my_piece(name), send, recv, (1 - grp, bat)).start()
+
+            return
+
+        @pl.when(goes_to(name))
+        def _():
+            if stage == 1:
+                piece = my_piece(name)
+                for ahead in range(1, depth):
+                    to = (lax.rem(lay + ahead, depth) * across + col) * 2 + core
+                    remote(piece, piece, send, recv, (grp, to)).start()
+            elif stage == 2:
+                piece = buf.at[core, col]
+                for ahead in range(1, across):
+                    to = (lay * across + lax.rem(col + ahead, across)) * 2 + core
+                    remote(piece, piece, send, recv, (grp, to)).start()
+            else:
+                piece = buf.at[core]
+                remote(piece, piece, send, recv, (grp, sibling)).start()
+
+    def size_waits(name, stage, side):
+        buf = gathered[name]
+        sem = sems(name, stage)[side]
+        if stage == 0:
+            if name == FEW_ALL or name in TO_PASSAGE:
+
+                @pl.when(is_passage if (name == FEW_ALL) == (side == 0) else is_query)
+                def _():
+                    hold(sem, my_piece(name))
+
+            return
+
+        @pl.when(goes_to(name))
+        def _():
+            if stage == 1:
+                hold(sem, buf.at[core, col, pl.ds(0, depth - 1)])
+            elif stage == 2:
+                hold(sem, buf.at[core, pl.ds(0, across - 1)])
+            else:
+                hold(sem, buf.at[core])
+
+    def come(name, stage):
+        size_waits(name, stage, 1)
+
+    def sent(name):
+        for stage in range(4):
+            size_waits(name, stage, 0)
+
+    def step_on(name, stage):
+        come(name, stage - 1)
+        go(name, stage)
+
+    def few_go():
+        @pl.when(is_passage)
+        def _():
+            dst = r.few_all.at[LATE, core, col, lay]
+
+            def push(step, carry):
+                other = lax.rem(bat + 2 * step, members)
+                remote(r.few_out.at[LATE], dst, r.f_send.at[0], r.f_recv.at[0], (0, other)).start()
+                return carry
+
+            lax.fori_loop(0, members // 2, push, 0)
+
+    def few_turn():
+        whole = r.few_all.at[LATE, core]
+        hold(r.f_recv.at[0], whole)
+        remote(whole, whole, r.f_send.at[1], r.f_recv.at[1], (grp, sibling)).start()
+
+    def few_come():
+        @pl.when(is_query)
+        def _():
+            hold(r.f_recv.at[1], r.few_all.at[LATE, core])
+
+        come(LAST_ALL, 3)
+
+    def few_sent():
+        @pl.when(is_query)
+        def _():
+            hold(r.f_send.at[1], r.few_all.at[LATE, core])
+
+        @pl.when(is_passage)
+        def _():
+            hold(r.f_send.at[0], r.few_all.at[LATE, core])
+
+    def share_rows(member):
+        return pl.ds(pl.multiple_of(member * share, share), share)
+
+    def spread(src, dst, at, to_grp, first_step, end_step=members):
+        send, recv = r.a_send.at[at], r.a_recv.at[at]
+
+        def push(step, carry):
+            other = lax.rem(bat + step, members)
+            remote(src(share_rows(other)), dst(my_slot), send, recv, (to_grp, other)).start()
+            return carry
+
+        lax.fori_loop(first_step, end_step, push, 0)
+
+    def spread_t(first_step, end_step):
+        spread(lambda rows: r.t_side.at[:, rows], lambda slot: r.side_got.at[slot], 0, 0, first_step, end_step)
+
+    def sum_peer(step):
+        if step == 0:
+            return (1 - grp, bat)
+        if step in (1, 2):
+            other = lay + 1 - 2 * lax.rem(lay, 2) if step == 1 else lax.rem(lay + 2, depth)
+            return (grp, (other * across + col) * 2 + core)
+        if step == 3:
+            return (grp, (lay * across + 1 - col) * 2 + core)
+        return (grp, sibling)
+
+    def sum_go(step):
+        remote(
+            r.sum_out.at[step], r.sum_in.at[step], r.v_send.at[step], r.v_recv.at[step], sum_peer(step)
+        ).start()
+
+    def sum_come(step):
+        hold(r.v_recv.at[step], r.sum_in.at[step])
+        r.sum_out[step + 1] = r.sum_out[step] + r.sum_in[step]
+
+    load(TOKENS).wait()
+    for at in (W_VALUE, W_OUT, W_IN, W_BACK):
+        load(at).start()
+    for copy in vector_loads:
+        copy.wait()
+    for at in range(len(vectors)):
+        r.rows_v[at : at + 1, :] = r.vectors_v[at].reshape(1, width)
+    r.b_in_v[...] = r.b_in_1d[...].reshape(1, hidden)
+    place_col, _ = listed(iota((cand, 1), 0))
+    _, seg_col = listed(iota((lanes, 1), 0) & (cand - 1))
+    tokens_v = r.tokens_v
+    pick = low(jnp.where(iota((cand, rows), 1) == place_col, 1.0, 0.0))
+    r.left[2 * lanes : 2 * lanes + cand, :] = pick
+    r.left[2 * lanes + cand : 2 * lanes + 2 * cand, :] = pick
+    x_cls = nn(pick, tokens_v[...])
+    x_low = low(x_cls)
+    keep(X_ALL, x_low)
+    pl.semaphore_wait(barrier, 2 * members - 1)
+    go(X_ALL, 1)
+    load(W_QUERY).wait()
+    load(W_KEY).wait()
+    q_cls = by_head(low(nn(x_low, r.w_query_v[...]) + vec(B_QUERY)))
+    key_query = low(nt(q_cls, r.w_key_v[...]) * HD ** (-0.5))
+    r.right[lanes : 2 * lanes, :] = key_query
+    scores = nt(key_query, tokens_v[...])
+    scores = jnp.where(seg_col == key_segment, scores, -1e30)
+    raised = jnp.exp(scores - jnp.max(scores, axis=-1, keepdims=True))
+    prob = raised / jnp.sum(raised, axis=-1, keepdims=True)
+    r.prob[...] = prob
+    r.left[0:lanes, :] = low(prob)
+    value_sum = nn(r.left[0:lanes, :], tokens_v[...])
+    @pl.when(is_query)
+    def _():
+        for v in range(lanes // 128):
+            r.u_side[v] = low(value_sum[128 * v : 128 * v + 128].T)
+        spread(lambda rows: r.u_side.at[pl.ds(0, 2), rows], lambda slot: r.side_got.at[slot, pl.ds(0, 2)], 4, 1, 0)
+
+    @pl.when(is_passage)
+    def _():
+        r.u_few[...] = few_rows(value_sum)
+        spread(lambda rows: r.u_few.at[rows], lambda slot: r.few_got.at[slot], 3, 1, 1)
+
+    load(W_VALUE).wait()
+    load(W_OUT).wait()
+    mixed = low(pick_heads(nn(low(value_sum), r.w_value_v[...])) + vec(B_VALUE))
+    keep(MIXED_ALL, mixed)
+    unit_one, rate_one = unit_rows(x_cls + nn(mixed, r.w_out_v[...]) + vec(B_OUT))
+    normed = unit_one * vec(GAIN_ATTN) + vec(SHIFT_ATTN)
+    normed_low = low(normed)
+    keep(NORMED_ALL, normed_low)
+    r.unit_one[...] = unit_one
+    r.rate_one[...] = rate_one
+    load(W_IN).wait()
+    load(W_BACK).wait()
+    active, slope = gelu_both(nn(normed_low, r.w_in_v[...]) + r.b_in_v[...])
+    r.slope[...] = slope
+    unit_two, rate_two = unit_rows(normed + nn(low(active), r.w_back_v[...]) + vec(B_BACK))
+    r.unit_two[...] = unit_two
+    r.rate_two[...] = rate_two
+    cls = low(unit_two * vec(GAIN_FFN) + vec(SHIFT_FFN))
+    r.cls[...] = cls
+
+
+    per_core = (groups - 1) * members // 2
+    lanes_n = 2 * per_core * 8
+
+    @pl.when(is_passage)
+    def _():
+        r.pas_out[...] = pack_eight(cls[0:8])
+
+        def push(k, carry):
+            at = (grp - 1) * (members // 2) + lax.div(bat, 2)
+            remote(
+                r.pas_out, r.pas_in.at[core, at], r.b_send.at[0], r.b_recv.at[0], (0, 2 * k + core)
+            ).start()
+            return carry
+
+        lax.fori_loop(0, members // 2, push, 0)
+
+    for name in (NORMED_ALL, MIXED_ALL):
+        go(name, 0)
+    go(FEW_ALL, 0)
+
+
+    def rank_rows():
+        hold(r.b_recv.at[0], r.pas_in.at[core])
+        mine = r.pas_in.at[core]
+        remote(mine, mine, r.b_send.at[1], r.b_recv.at[1], (grp, sibling)).start()
+        pos_col = jnp.zeros((cand, 1), jnp.int32)
+        row = iota((cand, 1), 0)
+        for s in range(cand):
+            pos_col = jnp.where(row == s, r.positives[bat * cand + s], pos_col)
+        spot = iota((1, lanes_n), 1)
+        within = spot & 7
+        owner = spot >> 3
+        owner_core = lax.div(owner, per_core)
+        owner = owner - owner_core * per_core
+        owner_grp = lax.div(owner, members // 2)
+        owner = (owner - owner_grp * (members // 2)) * 2 + owner_core + owner_grp * members
+        real = within < PAS_DEV
+        number = jnp.where(real, owner * PAS_DEV + within, -1)
+        hold(r.b_recv.at[1], r.pas_in.at[1 - core])
+        passages = low(unpack_eight(r.pas_in[...].reshape(2 * per_core, PART, half)))
+        queries = r.cls[...]
+        ranks = jnp.where(real, nt(queries, passages) * score_scale, -1e30)
+        grown = jnp.exp(ranks - jnp.max(ranks, axis=-1, keepdims=True))
+        soft = grown / jnp.sum(grown, axis=-1, keepdims=True)
+        rank_grad = low(jnp.where(real, soft - jnp.where(number == pos_col, 1.0, 0.0), 0.0))
+        r.y_grad[...] = nn(rank_grad, passages) * score_scale
+        terms = (tn(rank_grad, queries) * score_scale).reshape(2 * per_core, 8, width)
+        r.pas_part[...] = low(
+            jnp.concatenate([terms[:, :, :half], terms[:, :, half:]], axis=1)
+        ).reshape(2, per_core, PART, half)
+        remote(
+            r.pas_part.at[1 - core], r.pas_twin, r.b_send.at[2], r.b_recv.at[2], (grp, sibling)
+        ).start()
+        hold(r.b_recv.at[2], r.pas_twin)
+        r.pas_sum[...] = low(wide(r.pas_part[core]) + wide(r.pas_twin[...]))
+
+        def push(at, carry):
+            to = (1 + lax.div(at, members // 2), 2 * lax.rem(at, members // 2) + core)
+            remote(
+                r.pas_sum.at[at], r.pas_got.at[lax.div(bat, 2)], r.b_send.at[3], r.b_recv.at[3], to
+            ).start()
+            return carry
+
+        lax.fori_loop(0, per_core, push, 0)
+
+    def passage_rows():
+        hold(r.b_recv.at[3], r.pas_got)
+        total = jnp.sum(wide(r.pas_got[...]), axis=0)
+        r.y_grad[0:8, :] = jnp.concatenate([total[0:8], total[8:16]], axis=1)
+        r.y_grad[8:cand, :] = jnp.zeros((cand - 8, width), jnp.float32)
+
+    def backward_rows():
+        y_grad = r.y_grad[...]
+        unit = r.unit_two[...]
+        gain_sum = jnp.sum(y_grad * unit, axis=0, keepdims=True)
+        shift_sum = jnp.sum(y_grad, axis=0, keepdims=True)
+        two_grad = norm_back(y_grad, unit, r.rate_two[...], vec(GAIN_FFN))
+        branch = low(two_grad)
+        keep(BRANCH_ALL, branch)
+        go(BRANCH_ALL, 0)
+
+        @pl.when(is_query)
+        def _():
+            go(BRANCH_ALL, 1)
+
+        pre_grad = low(nt(branch, r.w_back_v[...]) * r.slope[...])
+        pre_sum = jnp.sum(wide(pre_grad), axis=0, keepdims=True)
+        normed_grad = two_grad + nt(pre_grad, r.w_in_v[...])
+        unit = r.unit_one[...]
+        gain_one = jnp.sum(normed_grad * unit, axis=0, keepdims=True)
+        shift_one = jnp.sum(normed_grad, axis=0, keepdims=True)
+        one_grad = norm_back(normed_grad, unit, r.rate_one[...], vec(GAIN_ATTN))
+        attn = low(one_grad)
+        keep(ATTN_ALL, attn)
+        go(ATTN_ALL, 0)
+        mixed_low = low(nt(attn, r.w_out_v[...]))
+        mixed_grad = by_head(mixed_low)
+        value_mix = low(nt(mixed_grad, r.w_value_v[...]))
+        r.right[0:lanes, :] = value_mix
+        prob_grad = nt(value_mix, tokens_v[...])
+        prob = r.prob[...]
+        score_grad = low(prob * (prob_grad - jnp.sum(prob * prob_grad, axis=-1, keepdims=True)))
+        r.left[lanes : 2 * lanes, :] = score_grad
+        token_sum = nn(score_grad, tokens_v[...])
+        query_grad = low(pick_heads(nn(low(token_sum), r.w_key_v[...])) * HD ** (-0.5))
+        keep(QUERY_ALL, query_grad)
+        go(QUERY_ALL, 1)
+        few_go()
+        r.t_sum[...] = token_sum
+        col_sums = [jnp.sum(wide(v), axis=0, keepdims=True) for v in (query_grad, mixed_low, attn, branch)]
+        r.sum_out[0] = jnp.concatenate(
+            [gain_sum, shift_sum, gain_one, shift_one]
+            + col_sums
+            + [pre_sum[:, width * j : width * (j + 1)] for j in range(hidden // width)]
+            + [jnp.zeros((8 - hidden // width, width), jnp.float32)],
+            axis=0,
+        )
+        sum_go(0)
+
+        @pl.when(is_query)
+        def _():
+            remote(r.u_side.at[2], r.u_twin, r.a_send.at[2], r.a_recv.at[2], (1, bat)).start()
+
+        row_grad = one_grad + nt(query_grad, r.w_query_v[...])
+        row_high = low(row_grad)
+        r.right[2 * lanes : 2 * lanes + cand, :] = row_high
+        r.right[2 * lanes + cand : 2 * lanes + 2 * cand, :] = low(row_grad - wide(row_high))
+        pltpu.make_async_copy(r.left, r.left_out, r.store_sem.at[1]).start()
+        pltpu.make_async_copy(r.right, r.right_out, r.store_sem.at[2]).start()
+
+    tile = 256
+    tiles = rows // tile
+    first_half = iota((1, 128), 1) < HD
+    half_on = low(jnp.where(first_half, 1.0, 0.0))
+    half_off = low(jnp.where(first_half, 0.0, 1.0))
+    one_lanes = jnp.full((tile, 128), 1.0, jnp.bfloat16)
+
+    def attend_tile(i):
+        at = pl.multiple_of(i * tile, tile)
+        tok = tokens_v[pl.ds(at, tile), :]
+        query = low(nn(tok, r.w_query_v[...]) + vec(B_QUERY)) * jnp.bfloat16(HD ** (-0.5))
+        key = low(nn(tok, r.w_key_v[...]))
+        value = low(nn(tok, r.w_value_v[...]) + vec(B_VALUE))
+        token_col = iota((tile, 1), 0) + at
+        bucket = jnp.where(i < BLK // tile, first, second)
+        segment, _ = segment_of(token_col, bucket)
+        unseen = jnp.where(segment == r.key_seg[i], 0.0, -1e30)
+        outs = []
+        for pair in range(H // 2):
+            span = slice(128 * pair, 128 * pair + 128)
+            q_pair, k_pair, v_pair = query[:, span], key[:, span], value[:, span]
+            value_one = jnp.concatenate([v_pair, one_lanes], axis=1)
+            parts = []
+            for side in (half_on, half_off):
+                s = nt(q_pair * side, k_pair) + unseen
+                e = jnp.exp(s - jnp.max(s, axis=-1, keepdims=True))
+                both = nn(low(e), value_one)
+                parts.append(both[:, :128] / both[:, 128:])
+            outs.append(low(jnp.where(first_half, parts[0], parts[1])))
+        mixed_tile = jnp.concatenate(outs, axis=1)
+        unit_tile, _ = unit_rows(wide(tok) + nn(mixed_tile, r.w_out_v[...]) + vec(B_OUT))
+        r.normed_v[...] = unit_tile * vec(GAIN_ATTN) + vec(SHIFT_ATTN)
+
+    def feed_tile(i):
+        at = pl.multiple_of(i * tile, tile)
+        normed_tile = r.normed_v[...]
+        low_tile = low(normed_tile)
+        total = normed_tile + vec(B_BACK)
+        span = hidden // 4
+        pre = nn(low_tile, r.w_in_v[:, 0:span]) + r.b_in_v[:, 0:span]
+        for j in range(4):
+            ahead = slice((j + 1) * span, (j + 2) * span)
+            if j < 3:
+                later = nn(low_tile, r.w_in_v[:, ahead]) + r.b_in_v[:, ahead]
+            total = total + nn(low(gelu(pre)), r.w_back_v[j * span : (j + 1) * span, :])
+            pre = later
+        unit_tile, _ = unit_rows(total)
+        r.enc_v[pl.ds(at, tile), :] = low(unit_tile * vec(GAIN_FFN) + vec(SHIFT_FFN))
+        spot = pl.ds(at, tile)
+        pltpu.make_async_copy(r.enc_v.at[spot], r.encoded.at[spot], r.store_sem.at[0]).start()
+
+    def sum_step(step):
+        def act():
+            sum_come(step - 1)
+            sum_go(step)
+
+        return act
+
+    def stage_step(name, stage):
+        return lambda: step_on(name, stage)
+
+    def twin_spread():
+        hold(r.a_recv.at[2], r.u_twin)
+        spread(lambda rows: r.u_twin.at[rows], lambda slot: r.side_got.at[slot, 2], 5, 1, 1)
+
+    def many_spread():
+        for v in range(lanes // 128):
+            r.t_side[v] = low(r.t_sum[128 * v : 128 * v + 128].T)
+        spread_t(1, members)
+
+    def few_spread():
+        r.t_few[...] = few_rows(r.t_sum[...])
+        spread(lambda rows: r.t_few.at[rows], lambda slot: r.few_got.at[slot], 1, 0, 0)
+
+    QUERY_MOVES = {
+        0: [stage_step(NORMED_ALL, 2), stage_step(X_ALL, 3)],
+        2: [stage_step(BRANCH_ALL, 2), stage_step(NORMED_ALL, 3)],
+        3: [sum_step(1), stage_step(FEW_ALL, 1), stage_step(QUERY_ALL, 2)],
+        4: [sum_step(2), many_spread, stage_step(BRANCH_ALL, 3)],
+        5: [few_turn, stage_step(FEW_ALL, 2)],
+        6: [sum_step(3), stage_step(FEW_ALL, 3)],
+        7: [sum_step(4)],
+        8: [stage_step(QUERY_ALL, 3)],
+    }
+    PASSAGE_MOVES = {
+        1: [stage_step(NORMED_ALL, 1), lambda: go(FEW_ALL, 1)],
+        2: [sum_step(1), lambda: go(LAST_ALL, 1), stage_step(NORMED_ALL, 2)],
+        3: [stage_step(ATTN_ALL, 1), stage_step(FEW_ALL, 2)],
+        4: [sum_step(2), stage_step(MIXED_ALL, 2), stage_step(NORMED_ALL, 3)],
+        5: [twin_spread, few_spread, stage_step(LAST_ALL, 2), stage_step(BRANCH_ALL, 2), stage_step(FEW_ALL, 3)],
+        6: [stage_step(MIXED_ALL, 3)],
+        7: [sum_step(3), stage_step(LAST_ALL, 3), stage_step(BRANCH_ALL, 3), stage_step(ATTN_ALL, 2)],
+        8: [],
+    }
+
+    def moves(i, odd):
+        for table, where in ((QUERY_MOVES, is_query), (PASSAGE_MOVES, is_passage)):
+            for point, acts in table.items():
+                if point // 2 < tiles and point % 2 == odd:
+
+                    @pl.when(jnp.logical_and(i == point // 2, where))
+                    def _():
+                        for act in acts:
+                            act()
+
+    def turn(i, carry):
+        attend_tile(i)
+
+        @pl.when(jnp.logical_and(i == 0, is_query))
+        def _():
+            rank_rows()
+            go(NORMED_ALL, 1)
+            step_on(X_ALL, 2)
+
+        @pl.when(jnp.logical_and(i == 1, is_passage))
+        def _():
+            passage_rows()
+            step_on(BRANCH_ALL, 1)
+            step_on(MIXED_ALL, 1)
+
+        @pl.when(i == jnp.where(is_query, 0, 1))
+        def _():
+            backward_rows()
+
+        moves(i, 0)
+        feed_tile(i)
+        moves(i, 1)
+        return carry
+
+    lax.fori_loop(0, tiles, turn, 0)
+
+    for table, where in ((QUERY_MOVES, is_query), (PASSAGE_MOVES, is_passage)):
+
+        @pl.when(where)
+        def _():
+            for act in table[2 * tiles]:
+                act()
+
+
+    def flatten(name, dst):
+        rows_q = gathered[name][...].reshape(slots, 2 * cand, half)
+        dst[0:query_rows, 0:half] = rows_q[:, 0:cand].reshape(query_rows, half)
+        dst[0:query_rows, half:width] = rows_q[:, cand : 2 * cand].reshape(query_rows, half)
+        when, at = divmod((TO_QUERY if name in TO_QUERY else TO_PASSAGE).index(name), 2)
+        rows_p = r.few_all[when, :, :, :, PART * at : PART * at + PART].reshape(slots, PART, half)
+        dst[query_rows:all_rows, :] = low(unpack_eight(rows_p))
+
+    win = 256
+    at48 = bat * share
+    base48 = jnp.minimum(lax.div(at48, 128) * 128, width - win)
+    off48 = pl.multiple_of(at48 - base48, 8)
+    win48 = pl.ds(pl.multiple_of(base48, 128), win)
+    share_in = hidden // members
+    at192 = bat * share_in
+    base192 = jnp.minimum(lax.div(at192, 128) * 128, hidden - win)
+    off192 = pl.multiple_of(at192 - base192, 8)
+    win192 = pl.ds(pl.multiple_of(base192, 128), win)
+    mine48 = pl.ds(off48, share)
+    side = hidden // 2
+    own_side = pl.multiple_of(grp * side, 128)
+    other_side = pl.multiple_of((1 - grp) * side, 128)
+
+    def swap(at, src):
+        remote(src, (r.swap_in0, r.swap_in1)[at], r.s_send.at[at], r.s_recv.at[at], (1 - grp, bat)).start()
+
+    come(FEW_ALL, 3)
+    few_come()
+    come(NORMED_ALL, 3)
+    flatten(NORMED_ALL, r.flat_a)
+    come(BRANCH_ALL, 3)
+    flatten(BRANCH_ALL, r.flat_b)
+    step = side // 2
+
+    def slope_cols(j, carry):
+        span = pl.ds(pl.multiple_of(own_side + j * step, 128), step)
+        slope_j = gelu_slope(nn(r.flat_a[...], r.w_in_v[:, span]) + r.b_in_v[:, span])
+        pre_j = low(nt(r.flat_b[...], r.w_back_v[span, :]) * slope_j)
+        here = pl.ds(pl.multiple_of(j * step, 128), step)
+        r.stage[:, here] = tn(r.flat_a[:, win48], pre_j)
+        return carry
+
+    lax.fori_loop(0, 2, slope_cols, 0)
+    piece = low(r.stage[mine48, :])
+    r.swap_out0[...] = piece
+    swap(0, r.swap_out0)
+    r.g_in[:, pl.ds(own_side, side)] = wide(piece)
+    @pl.when(is_passage)
+    def _():
+        sum_step(4)()
+        step_on(ATTN_ALL, 3)
+
+    active_win = low(gelu(nn(r.flat_a[...], r.w_in_v[:, win192]) + r.b_in_v[:, win192]))
+    r.stage[:, 0:width] = tn(active_win, r.flat_b[...])
+    r.g_back[...] = r.stage[pl.ds(off192, share_in), 0:width]
+
+    def one_share(at, left, right):
+        r.stage[:, 0:width] = tn(left[:, win48], right[...])
+        r.swap_out1[at] = low(r.stage[mine48, 0:width])
+
+    @pl.when(is_query)
+    def _():
+        come(X_ALL, 3)
+        flatten(X_ALL, r.flat_c)
+        come(QUERY_ALL, 3)
+        flatten(QUERY_ALL, r.flat_d)
+        one_share(0, r.flat_c, r.flat_d)
+        r.factor[...] = (nn(r.flat_c[...], r.w_query_v[...]) + vec(B_QUERY)) * HD ** (-0.5)
+        r.side_got[my_slot] = r.t_side[:, share_rows(bat)]
+        hold(r.a_recv.at[0], r.side_got.at[pl.ds(0, members - 1)])
+        hold(r.a_recv.at[1], r.few_got)
+
+    @pl.when(is_passage)
+    def _():
+        come(MIXED_ALL, 3)
+        flatten(MIXED_ALL, r.flat_c)
+        come(ATTN_ALL, 3)
+        flatten(ATTN_ALL, r.flat_d)
+        one_share(0, r.flat_c, r.flat_d)
+        r.factor[...] = nt(r.flat_d[...], r.w_out_v[...])
+        r.side_got[my_slot, 2] = r.u_twin[share_rows(bat)]
+        r.few_got[my_slot] = r.u_few[share_rows(bat)]
+        hold(r.a_recv.at[4], r.side_got.at[:, pl.ds(0, 2)])
+        hold(r.a_recv.at[5], r.side_got.at[pl.ds(0, members - 1), 2])
+        hold(r.a_recv.at[3], r.few_got.at[pl.ds(0, members - 1)])
+
+    head_4 = iota((1, HEADS_VREG, 1, HEADS_VREG * HD), 1)
+    lane_4 = iota((1, HEADS_VREG, 1, HEADS_VREG * HD), 3) >> 6
+    head_16 = iota((1, 16, 1, HEADS_VREG * HD), 1)
+    lane_16 = iota((1, 16, 1, HEADS_VREG * HD), 3) >> 6
+    few = jnp.concatenate([r.few_got[m] for m in range(slots)], axis=1)
+    for v in range(H // HEADS_VREG):
+        span = slice(256 * v, 256 * v + 256)
+        left = jnp.concatenate([r.side_got[m, v] for m in range(slots)], axis=1)
+        full = r.factor[0:query_rows, span].reshape(slots, 1, cand, 256)
+        right = low(jnp.where(head_4 == lane_4, full, 0.0)).reshape(slots * 128, 256)
+        total = nn(left, right)
+        full = r.factor[query_rows:all_rows, span].reshape(slots, 1, 8, 256)
+        right = low(jnp.where(head_16 == lane_16 + HEADS_VREG * v, full, 0.0)).reshape(slots * 128, 256)
+        r.swap_out1[1, :, span] = low(total + nn(few, right))
+    swap(1, r.swap_out1)
+
+    @pl.when(is_query)
+    def _():
+        r.g_query[...] = wide(r.swap_out1[0])
+        r.g_key[...] = wide(r.swap_out1[1])
+
+    @pl.when(is_passage)
+    def _():
+        r.g_out[...] = wide(r.swap_out1[0])
+        r.g_value[...] = wide(r.swap_out1[1])
+
+    sum_come(4)
+    mine = pltpu.roll(r.sum_out[5, 0:8], lax.rem(width - at48, width), 1)
+    shares = (
+        r.g_gain_ffn,
+        r.g_shift_ffn,
+        r.g_gain_attn,
+        r.g_shift_attn,
+        r.gb_query,
+        r.gb_value,
+        r.gb_out,
+        r.gb_back,
+    )
+    for at, ref in enumerate(shares):
+        ref[...] = mine[at : at + 1, 0:share].reshape(share)
+    line = r.sum_out[5, pl.ds(8 + lax.div(at192, width), 1), :]
+    line = pltpu.roll(
+        jnp.broadcast_to(line, (8, width)), lax.rem(width - lax.rem(at192, width), width), 1
+    )
+    r.gb_in[...] = line[0:1, 0:share_in].reshape(share_in)
+
+    hold(r.s_recv.at[0], r.swap_in0)
+    r.g_in[:, pl.ds(other_side, side)] = wide(r.swap_in0[...])
+    hold(r.s_recv.at[1], r.swap_in1)
+
+    @pl.when(is_query)
+    def _():
+        r.g_out[...] = wide(r.swap_in1[0])
+        r.g_value[...] = wide(r.swap_in1[1])
+
+    @pl.when(is_passage)
+    def _():
+        r.g_query[...] = wide(r.swap_in1[0])
+        r.g_key[...] = wide(r.swap_in1[1])
+
+    hold(r.store_sem.at[0], r.enc_v)
+    hold(r.store_sem.at[1], r.left)
+    hold(r.store_sem.at[2], r.right)
+    for name in range(len(gathered)):
+        sent(name)
+    few_sent()
+    for at in range(5):
+        hold(r.v_send.at[at], r.sum_out.at[at])
+    hold(r.s_send.at[0], r.swap_out0)
+    hold(r.s_send.at[1], r.swap_out1)
+
+    @pl.when(is_query)
+    def _():
+        hold(r.a_send.at[0], r.side_got.at[pl.ds(0, members - 1)])
+        hold(r.a_send.at[2], r.u_twin)
+        hold(r.a_send.at[4], r.side_got.at[:, pl.ds(0, 2)])
+        hold(r.b_send.at[1], r.pas_in.at[core])
+        hold(r.b_send.at[2], r.pas_twin)
+        hold(r.b_send.at[3], r.pas_sum)
+
+    @pl.when(is_passage)
+    def _():
+        hold(r.a_send.at[1], r.few_got)
+        hold(r.a_send.at[3], r.few_got.at[pl.ds(0, members - 1)])
+        hold(r.a_send.at[5], r.side_got.at[pl.ds(0, members - 1), 2])
+        hold(r.b_send.at[0], r.pas_got)
+
+
+def result_kernel(count, *refs):
+    ins, outs = refs[: count + 1], refs[count + 1 : 2 * count + 1]
+    held, (tile_out, load_sem, store_sem, grad_sem) = refs[2 * count + 1 : -4], refs[-4:]
+    loads = [pltpu.make_async_copy(src, dst, load_sem.at[at]) for at, (src, dst) in enumerate(zip(ins, held))]
+    for at in (1, 2, 0) + tuple(range(3, count + 1)):
+        loads[at].start()
+    places = (0,) + tuple(range(2, count))
+    stores = [
+        pltpu.make_async_copy(held[at + 1 if at else 0], outs[at], store_sem.at[at]) for at in places
+    ]
+    loads[1].wait()
+    loads[2].wait()
+    tile = tile_out.shape[0] // 4
+    grads = []
+    for i in range(4):
+        spot = slice(i * tile, (i + 1) * tile)
+        tile_out[spot, :] = tn(held[1][:, spot], held[2][...])
+        grads.append(pltpu.make_async_copy(tile_out.at[spot], outs[1].at[spot], grad_sem.at[i]))
+        grads[-1].start()
+        if i == 0:
+            for at, store in zip(places, stores):
+                loads[at + 1 if at else 0].wait()
+                store.start()
+    for copy in grads + stores:
+        copy.wait()
+
+
+def make_shards(groups, members):
+    def shards(*args):
+        tokens = args[0]
+        rows, width = tokens.shape
+        hidden = Ins(*args).w_in.shape[1]
+        share, share_in = width // members, hidden // members
+        cand = rows // QLEN
+        lanes = H * cand
+        all_rows = members * (cand + 8)
+        per_core = (groups - 1) * members // 2
+        across = members // 8
+        half = width // 2
+        f32, bf16 = jnp.float32, jnp.bfloat16
+        out_shapes = Outs(
+            encoded=((rows, width), bf16),
+            left_out=((2 * lanes + 2 * cand, rows), bf16),
+            right_out=((2 * lanes + 2 * cand, width), bf16),
+            g_query=((share, width), f32),
+            gb_query=((share,), f32),
+            g_key=((share, width), f32),
+            g_value=((share, width), f32),
+            gb_value=((share,), f32),
+            g_out=((share, width), f32),
+            gb_out=((share,), f32),
+            g_gain_attn=((share,), f32),
+            g_shift_attn=((share,), f32),
+            g_in=((share, hidden), f32),
+            gb_in=((share_in,), f32),
+            g_back=((share_in, width), f32),
+            gb_back=((share,), f32),
+            g_gain_ffn=((share,), f32),
+            g_shift_ffn=((share,), f32),
+        )
+        out_shape = tuple(jax.ShapeDtypeStruct(*pair) for pair in out_shapes)
+        dma = pltpu.SemaphoreType.DMA
+        gathered = pltpu.VMEM((2, across, 4, 2 * cand, half), bf16)
+        scratch = Scratch(
+            tokens_v=pltpu.VMEM((rows, width), bf16),
+            w_query_v=pltpu.VMEM((width, width), bf16),
+            w_key_v=pltpu.VMEM((width, width), bf16),
+            w_value_v=pltpu.VMEM((width, width), bf16),
+            w_out_v=pltpu.VMEM((width, width), bf16),
+            w_in_v=pltpu.VMEM((width, hidden), bf16),
+            w_back_v=pltpu.VMEM((hidden, width), bf16),
+            vectors_v=pltpu.VMEM((8, width), f32),
+            b_in_1d=pltpu.VMEM((hidden,), f32),
+            vector_sem=dma((9,)),
+            rows_v=pltpu.VMEM((8, width), f32),
+            t_sum=pltpu.VMEM((lanes, width), f32),
+            b_in_v=pltpu.VMEM((1, hidden), f32),
+            key_seg=pltpu.VMEM((rows // 256, 1, 256), jnp.int32),
+            left=pltpu.VMEM((2 * lanes + 2 * cand, rows), bf16),
+            right=pltpu.VMEM((2 * lanes + 2 * cand, width), bf16),
+            prob=pltpu.VMEM((lanes, rows), f32),
+            slope=pltpu.VMEM((cand, hidden), f32),
+            unit_one=pltpu.VMEM((cand, width), f32),
+            rate_one=pltpu.VMEM((cand, 1), f32),
+            unit_two=pltpu.VMEM((cand, width), f32),
+            rate_two=pltpu.VMEM((cand, 1), f32),
+            cls=pltpu.VMEM((cand, width), bf16),
+            y_grad=pltpu.VMEM((cand, width), f32),
+            x_all=gathered,
+            mixed_all=gathered,
+            normed_all=gathered,
+            branch_all=gathered,
+            attn_all=gathered,
+            query_all=gathered,
+            few_all=pltpu.VMEM((2, 2, across, 4, 2 * PART, half), bf16),
+            few_out=pltpu.VMEM((2, 2 * PART, half), bf16),
+            t_side=pltpu.VMEM((lanes // 128, width, 128), bf16),
+            u_side=pltpu.VMEM((lanes // 128, width, 128), bf16),
+            u_twin=pltpu.VMEM((width, 128), bf16),
+            t_few=pltpu.VMEM((width, 128), bf16),
+            u_few=pltpu.VMEM((width, 128), bf16),
+            side_got=pltpu.VMEM((members, lanes // 128, share, 128), bf16),
+            few_got=pltpu.VMEM((members, share, 128), bf16),
+            sum_out=pltpu.VMEM((6, 16, width), f32),
+            sum_in=pltpu.VMEM((5, 16, width), f32),
+            pas_out=pltpu.VMEM((PART, half), bf16),
+            pas_in=pltpu.VMEM((2, per_core, PART, half), bf16),
+            pas_part=pltpu.VMEM((2, per_core, PART, half), bf16),
+            pas_twin=pltpu.VMEM((per_core, PART, half), bf16),
+            pas_sum=pltpu.VMEM((per_core, PART, half), bf16),
+            pas_got=pltpu.VMEM((members // 2, PART, half), bf16),
+            normed_v=pltpu.VMEM((256, width), f32),
+            enc_v=pltpu.VMEM((rows, width), bf16),
+            flat_a=pltpu.VMEM((all_rows, width), bf16),
+            flat_b=pltpu.VMEM((all_rows, width), bf16),
+            flat_c=pltpu.VMEM((all_rows, width), bf16),
+            flat_d=pltpu.VMEM((all_rows, width), bf16),
+            factor=pltpu.VMEM((all_rows, width), f32),
+            stage=pltpu.VMEM((256, hidden // 2), f32),
+            swap_out0=pltpu.VMEM((share, hidden // 2), bf16),
+            swap_in0=pltpu.VMEM((share, hidden // 2), bf16),
+            swap_out1=pltpu.VMEM((2, share, width), bf16),
+            swap_in1=pltpu.VMEM((2, share, width), bf16),
+            load_sem=dma((7,)),
+            store_sem=dma((3,)),
+            g_send=dma((8, 4)),
+            g_recv=dma((8, 4)),
+            f_send=dma((2,)),
+            f_recv=dma((2,)),
+            v_send=dma((5,)),
+            v_recv=dma((5,)),
+            a_send=dma((6,)),
+            a_recv=dma((6,)),
+            b_send=dma((4,)),
+            b_recv=dma((4,)),
+            s_send=dma((2,)),
+            s_recv=dma((2,)),
+        )
+        anywhere = pl.BlockSpec(memory_space=pl.ANY)
+        vmem = pl.BlockSpec(memory_space=pltpu.VMEM)
+        smem = pl.BlockSpec(memory_space=pltpu.SMEM)
+        in_specs = [anywhere] * len(args)
+        for at in range(1, 4):
+            in_specs[at] = smem
+        out_specs = (anywhere,) * 3 + (vmem,) * (len(out_shape) - 3)
+        made = pl.pallas_call(
+            functools.partial(main_kernel, (groups, members, rows, width, hidden)),
+            out_shape=out_shape,
+            in_specs=in_specs,
+            out_specs=out_specs,
+            scratch_shapes=list(scratch),
+            name="layer",
+            compiler_params=pltpu.CompilerParams(
+                collective_id=0, has_side_effects=True, vmem_limit_bytes=60 * 1024 * 1024
+            ),
+        )(*args)
+        results = (out_shape[0], jax.ShapeDtypeStruct((rows, width), f32)) + out_shape[3:]
+        count = len(results)
+        return pl.pallas_call(
+            functools.partial(result_kernel, count),
+            out_shape=results,
+            in_specs=[anywhere] * (count + 1),
+            out_specs=(anywhere,) * count,
+            scratch_shapes=[pltpu.VMEM(shape.shape, shape.dtype) for shape in out_shape]
+            + [pltpu.VMEM((rows, width), f32), dma((count + 1,)), dma((count,)), dma((4,))],
+            name="results",
+            compiler_params=pltpu.CompilerParams(vmem_limit_bytes=60 * 1024 * 1024),
+        )(*made)
+
+    return shards
+
+
 def solution(mesh):
     in_specs = (
         P(("grp", "batch"), None),
@@ -363,4 +1558,7 @@
         P("batch"),
         P("batch"),
     )
+    groups, members = mesh.shape["grp"], mesh.shape["batch"]
+    fits = groups == 2 and members == 16
+    shards = make_shards(groups, members) if fits else plain_shards
     return jax.shard_map(shards, mesh=mesh, in_specs=in_specs, out_specs=out_specs, check_vma=False)

time: 937 us -> 83.4 us (0.09)
  waiting for transfers between devices: 476 us -> 0 us
  blocking collectives: 144 us -> 0 us
  local copies, waits for them, and re-layouts: 127 us -> 0 us
  matrix products: 116 us -> 0 us
  Pallas kernels: 0 us -> 82.3 us
  other arithmetic: 23.2 us -> 0 us
  starting transfers between devices: 20.6 us -> 0 us
  between operations: 17 us -> 0.85 us
    reduce_scatter x4 -> x0, waiting for transfers between devices: 361 us -> none  [the longest x1 116 us: shards(): lax.psum_scatter(w_back_grad, 'batch', scatter_dimension=0, tiled=True)]
    unnamed x2 -> x0, blocking collectives: 134 us -> none
    dot_general x35 -> x0, matrix products: 116 us -> none  [the longest x7 56.8 us: matmul(): return jnp.dot(left, right, preferred_element_type=jnp.float32)]
    unnamed x18 -> x0, waiting for transfers between devices: 84.8 us -> none
    pallas_call x0 -> x2, Pallas kernels: none -> 82.3 us  [the longest x1 76.6 us: shards(): pl.pallas_call(functools.partial(main_kernel, (groups, members, rows, wid...]
    unnamed x154 -> x0, local copies, waits for them, and re-layouts: 34.8 us -> none
    gather x16 -> x0, local copies, waits for them, and re-layouts: 34.2 us -> none  [the longest x1 5.45 us: shards(): kept_gelu, pull_gelu = jax.vjp(gelu_exact, hidden_pre[cand_rows])]
    all_gather x1 -> x0, waiting for transfers between devices: 30.3 us -> none  [shards(): lax.all_gather(cls_mine, ('grp', 'batch'), axis=0, tiled=True)]
  transfers between devices with their start and end apart: 16 -> 0, of which waited for: 7 -> 0; matrix products, arithmetic and copies ran while one was open for 9% -> 0% of each run, Pallas kernels for 0% -> 0%
where the time goes in v1:
time: 83.4 us; the launch traced here: 83.2 us
  Pallas kernels  82.3 us (99%)
  between operations  0.85 us (1%)
    pallas_call x1, Pallas kernels, shards(): pl.pallas_call(functools.partial(main_kernel, (groups, members, rows, wid...  76.6 us
    pallas_call x1, Pallas kernels, shards(): pl.pallas_call(functools.partial(result_kernel, count), out_shape=results...  5.73 us

profile of v1, /device:TPU:0, one launch (start us, length us, event | category | flops | bytes accessed | tf_op | source)
XLA Modules:
  0.0 83.2 jit_solution(1593655467558720202)
XLA Ops:
  0.7 76.6 %layer.1 = (bf16[1024,768]{1,0:T(8,128)(2,1)}, bf16[832,1024]{1,0:T(8,128)(2,1)}, bf16[832,768]{1,0:T(8,128)(2,1)}, f32[48,768]{1,0:T(8,128)}, f32[48]{0:T(128)}...) custom-call(bf16[1024,768]{1,0:T(8,128)(2,1)} %refs_0_.1, ...), custom_call_target="tpu_custom_call" | custom-call | tf_op jit(solution)/shard_map/layer/pallas_call | solution.py:1493
  77.3 5.7 %results.1 = (bf16[1024,768]{1,0:T(8,128)(2,1)}, f32[1024,768]{1,0:T(8,128)}, f32[48,768]{1,0:T(8,128)}, f32[48]{0:T(128)}, f32[48,768]{1,0:T(8,128)}, /*index=5...) custom-call(bf16[1024,768]{1,0:T(8,128)(2,1)} %get-tuple-element.35., ...), custom_call_target="tpu_custom_call" | custom-call | tf_op jit(solution)/shard_map/results/pallas_call | solution.py:1506

commit v2 on v1

--- a/solution.py
+++ b/solution.py
@@ -493,7 +493,7 @@
     t_few: typing.Any
     u_few: typing.Any
     side_got: typing.Any
-    few_got: typing.Any
+    t_twin: typing.Any
     sum_out: typing.Any
     sum_in: typing.Any
     pas_out: typing.Any
@@ -818,7 +818,7 @@
         lax.fori_loop(first_step, end_step, push, 0)
 
     def spread_t(first_step, end_step):
-        spread(lambda rows: r.t_side.at[:, rows], lambda slot: r.side_got.at[slot], 0, 0, first_step, end_step)
+        spread(lambda rows: r.t_side.at[:, rows], lambda slot: r.side_got.at[slot, pl.ds(0, 3)], 0, 0, first_step, end_step)
 
     def sum_peer(step):
         if step == 0:
@@ -879,7 +879,7 @@
     @pl.when(is_passage)
     def _():
         r.u_few[...] = few_rows(value_sum)
-        spread(lambda rows: r.u_few.at[rows], lambda slot: r.few_got.at[slot], 3, 1, 1)
+        spread(lambda rows: r.u_few.at[rows], lambda slot: r.side_got.at[slot, 3], 3, 1, 1)
 
     load(W_VALUE).wait()
     load(W_OUT).wait()
@@ -997,6 +997,7 @@
         attn = low(one_grad)
         keep(ATTN_ALL, attn)
         go(ATTN_ALL, 0)
+        go(LAST_ALL, 1)
         mixed_low = low(nt(attn, r.w_out_v[...]))
         mixed_grad = by_head(mixed_low)
         value_mix = low(nt(mixed_grad, r.w_value_v[...]))
@@ -1102,9 +1103,13 @@
             r.t_side[v] = low(r.t_sum[128 * v : 128 * v + 128].T)
         spread_t(1, members)
 
+    def few_push():
+        r.t_few[...] = few_rows(r.t_sum[...])
+        remote(r.t_few, r.t_twin, r.a_send.at[1], r.a_recv.at[1], (0, bat)).start()
+
     def few_spread():
-        r.t_few[...] = few_rows(r.t_sum[...])
-        spread(lambda rows: r.t_few.at[rows], lambda slot: r.few_got.at[slot], 1, 0, 0)
+        hold(r.a_recv.at[1], r.t_twin)
+        spread(lambda rows: r.t_twin.at[rows], lambda slot: r.side_got.at[slot, 3], 6, 0, 1)
 
     QUERY_MOVES = {
         0: [stage_step(NORMED_ALL, 2), stage_step(X_ALL, 3)],
@@ -1112,18 +1117,18 @@
         3: [sum_step(1), stage_step(FEW_ALL, 1), stage_step(QUERY_ALL, 2)],
         4: [sum_step(2), many_spread, stage_step(BRANCH_ALL, 3)],
         5: [few_turn, stage_step(FEW_ALL, 2)],
-        6: [sum_step(3), stage_step(FEW_ALL, 3)],
-        7: [sum_step(4)],
+        6: [few_spread, sum_step(3)],
+        7: [sum_step(4), stage_step(FEW_ALL, 3)],
         8: [stage_step(QUERY_ALL, 3)],
     }
     PASSAGE_MOVES = {
-        1: [stage_step(NORMED_ALL, 1), lambda: go(FEW_ALL, 1)],
-        2: [sum_step(1), lambda: go(LAST_ALL, 1), stage_step(NORMED_ALL, 2)],
-        3: [stage_step(ATTN_ALL, 1), stage_step(FEW_ALL, 2)],
-        4: [sum_step(2), stage_step(MIXED_ALL, 2), stage_step(NORMED_ALL, 3)],
-        5: [twin_spread, few_spread, stage_step(LAST_ALL, 2), stage_step(BRANCH_ALL, 2), stage_step(FEW_ALL, 3)],
-        6: [stage_step(MIXED_ALL, 3)],
-        7: [sum_step(3), stage_step(LAST_ALL, 3), stage_step(BRANCH_ALL, 3), stage_step(ATTN_ALL, 2)],
+        1: [stage_step(NORMED_ALL, 1)],
+        2: [sum_step(1), few_push, lambda: go(FEW_ALL, 1), stage_step(NORMED_ALL, 2)],
+        3: [stage_step(ATTN_ALL, 1), stage_step(BRANCH_ALL, 2)],
+        4: [sum_step(2), stage_step(MIXED_ALL, 1), stage_step(LAST_ALL, 2), stage_step(NORMED_ALL, 3)],
+        5: [twin_spread, stage_step(FEW_ALL, 2), stage_step(BRANCH_ALL, 3)],
+        6: [stage_step(ATTN_ALL, 2), stage_step(LAST_ALL, 3)],
+        7: [sum_step(3), stage_step(MIXED_ALL, 2), stage_step(FEW_ALL, 3)],
         8: [],
     }
 
@@ -1150,7 +1155,6 @@
         def _():
             passage_rows()
             step_on(BRANCH_ALL, 1)
-            step_on(MIXED_ALL, 1)
 
         @pl.when(i == jnp.where(is_query, 0, 1))
         def _():
@@ -1194,8 +1198,8 @@
     own_side = pl.multiple_of(grp * side, 128)
     other_side = pl.multiple_of((1 - grp) * side, 128)
 
-    def swap(at, src):
-        remote(src, (r.swap_in0, r.swap_in1)[at], r.s_send.at[at], r.s_recv.at[at], (1 - grp, bat)).start()
+    def swap(at, src, dst):
+        remote(src, dst, r.s_send.at[at], r.s_recv.at[at], (1 - grp, bat)).start()
 
     come(FEW_ALL, 3)
     few_come()
@@ -1216,20 +1220,25 @@
     lax.fori_loop(0, 2, slope_cols, 0)
     piece = low(r.stage[mine48, :])
     r.swap_out0[...] = piece
-    swap(0, r.swap_out0)
+    swap(0, r.swap_out0, r.swap_in0)
     r.g_in[:, pl.ds(own_side, side)] = wide(piece)
+    def back_share():
+        active_win = low(gelu(nn(r.flat_a[...], r.w_in_v[:, win192]) + r.b_in_v[:, win192]))
+        r.stage[:, 0:width] = tn(active_win, r.flat_b[...])
+        r.g_back[...] = r.stage[pl.ds(off192, share_in), 0:width]
+
     @pl.when(is_passage)
     def _():
         sum_step(4)()
         step_on(ATTN_ALL, 3)
-
-    active_win = low(gelu(nn(r.flat_a[...], r.w_in_v[:, win192]) + r.b_in_v[:, win192]))
-    r.stage[:, 0:width] = tn(active_win, r.flat_b[...])
-    r.g_back[...] = r.stage[pl.ds(off192, share_in), 0:width]
-
-    def one_share(at, left, right):
+        step_on(MIXED_ALL, 3)
+        back_share()
+
+
+    def one_share(left, right):
         r.stage[:, 0:width] = tn(left[:, win48], right[...])
-        r.swap_out1[at] = low(r.stage[mine48, 0:width])
+        r.swap_out1[0] = low(r.stage[mine48, 0:width])
+        swap(1, r.swap_out1.at[0], r.swap_in1.at[0])
 
     @pl.when(is_query)
     def _():
@@ -1237,11 +1246,12 @@
         flatten(X_ALL, r.flat_c)
         come(QUERY_ALL, 3)
         flatten(QUERY_ALL, r.flat_d)
-        one_share(0, r.flat_c, r.flat_d)
+        one_share(r.flat_c, r.flat_d)
         r.factor[...] = (nn(r.flat_c[...], r.w_query_v[...]) + vec(B_QUERY)) * HD ** (-0.5)
-        r.side_got[my_slot] = r.t_side[:, share_rows(bat)]
-        hold(r.a_recv.at[0], r.side_got.at[pl.ds(0, members - 1)])
-        hold(r.a_recv.at[1], r.few_got)
+        r.side_got[my_slot, 0:3] = r.t_side[:, share_rows(bat)]
+        r.side_got[my_slot, 3] = r.t_twin[share_rows(bat)]
+        hold(r.a_recv.at[0], r.side_got.at[pl.ds(0, members - 1), pl.ds(0, 3)])
+        hold(r.a_recv.at[6], r.side_got.at[pl.ds(0, members - 1), 3])
 
     @pl.when(is_passage)
     def _():
@@ -1249,19 +1259,19 @@
         flatten(MIXED_ALL, r.flat_c)
         come(ATTN_ALL, 3)
         flatten(ATTN_ALL, r.flat_d)
-        one_share(0, r.flat_c, r.flat_d)
+        one_share(r.flat_c, r.flat_d)
         r.factor[...] = nt(r.flat_d[...], r.w_out_v[...])
         r.side_got[my_slot, 2] = r.u_twin[share_rows(bat)]
-        r.few_got[my_slot] = r.u_few[share_rows(bat)]
+        r.side_got[my_slot, 3] = r.u_few[share_rows(bat)]
         hold(r.a_recv.at[4], r.side_got.at[:, pl.ds(0, 2)])
         hold(r.a_recv.at[5], r.side_got.at[pl.ds(0, members - 1), 2])
-        hold(r.a_recv.at[3], r.few_got.at[pl.ds(0, members - 1)])
+        hold(r.a_recv.at[3], r.side_got.at[pl.ds(0, members - 1), 3])
 
     head_4 = iota((1, HEADS_VREG, 1, HEADS_VREG * HD), 1)
     lane_4 = iota((1, HEADS_VREG, 1, HEADS_VREG * HD), 3) >> 6
     head_16 = iota((1, 16, 1, HEADS_VREG * HD), 1)
     lane_16 = iota((1, 16, 1, HEADS_VREG * HD), 3) >> 6
-    few = jnp.concatenate([r.few_got[m] for m in range(slots)], axis=1)
+    few = jnp.concatenate([r.side_got[m, 3] for m in range(slots)], axis=1)
     for v in range(H // HEADS_VREG):
         span = slice(256 * v, 256 * v + 256)
         left = jnp.concatenate([r.side_got[m, v] for m in range(slots)], axis=1)
@@ -1271,7 +1281,12 @@
         full = r.factor[query_rows:all_rows, span].reshape(slots, 1, 8, 256)
         right = low(jnp.where(head_16 == lane_16 + HEADS_VREG * v, full, 0.0)).reshape(slots * 128, 256)
         r.swap_out1[1, :, span] = low(total + nn(few, right))
-    swap(1, r.swap_out1)
+    swap(2, r.swap_out1.at[1], r.swap_in1.at[1])
+
+    @pl.when(is_query)
+    def _():
+        back_share()
+
 
     @pl.when(is_query)
     def _():
@@ -1305,7 +1320,8 @@
 
     hold(r.s_recv.at[0], r.swap_in0)
     r.g_in[:, pl.ds(other_side, side)] = wide(r.swap_in0[...])
-    hold(r.s_recv.at[1], r.swap_in1)
+    hold(r.s_recv.at[1], r.swap_in1.at[0])
+    hold(r.s_recv.at[2], r.swap_in1.at[1])
 
     @pl.when(is_query)
     def _():
@@ -1326,11 +1342,13 @@
     for at in range(5):
         hold(r.v_send.at[at], r.sum_out.at[at])
     hold(r.s_send.at[0], r.swap_out0)
-    hold(r.s_send.at[1], r.swap_out1)
+    hold(r.s_send.at[1], r.swap_out1.at[0])
+    hold(r.s_send.at[2], r.swap_out1.at[1])
 
     @pl.when(is_query)
     def _():
-        hold(r.a_send.at[0], r.side_got.at[pl.ds(0, members - 1)])
+        hold(r.a_send.at[0], r.side_got.at[pl.ds(0, members - 1), pl.ds(0, 3)])
+        hold(r.a_send.at[6], r.side_got.at[pl.ds(0, members - 1), 3])
         hold(r.a_send.at[2], r.u_twin)
         hold(r.a_send.at[4], r.side_got.at[:, pl.ds(0, 2)])
         hold(r.b_send.at[1], r.pas_in.at[core])
@@ -1339,8 +1357,8 @@
 
     @pl.when(is_passage)
     def _():
-        hold(r.a_send.at[1], r.few_got)
-        hold(r.a_send.at[3], r.few_got.at[pl.ds(0, members - 1)])
+        hold(r.a_send.at[1], r.t_few)
+        hold(r.a_send.at[3], r.side_got.at[pl.ds(0, members - 1), 3])
         hold(r.a_send.at[5], r.side_got.at[pl.ds(0, members - 1), 2])
         hold(r.b_send.at[0], r.pas_got)
 
@@ -1446,8 +1464,8 @@
             u_twin=pltpu.VMEM((width, 128), bf16),
             t_few=pltpu.VMEM((width, 128), bf16),
             u_few=pltpu.VMEM((width, 128), bf16),
-            side_got=pltpu.VMEM((members, lanes // 128, share, 128), bf16),
-            few_got=pltpu.VMEM((members, share, 128), bf16),
+            side_got=pltpu.VMEM((members, lanes // 128 + 1, share, 128), bf16),
+            t_twin=pltpu.VMEM((width, 128), bf16),
             sum_out=pltpu.VMEM((6, 16, width), f32),
             sum_in=pltpu.VMEM((5, 16, width), f32),
             pas_out=pltpu.VMEM((PART, half), bf16),
@@ -1476,12 +1494,12 @@
             f_recv=dma((2,)),
             v_send=dma((5,)),
             v_recv=dma((5,)),
-            a_send=dma((6,)),
-            a_recv=dma((6,)),
+            a_send=dma((7,)),
+            a_recv=dma((7,)),
             b_send=dma((4,)),
             b_recv=dma((4,)),
-            s_send=dma((2,)),
-            s_recv=dma((2,)),
+            s_send=dma((3,)),
+            s_recv=dma((3,)),
         )
         anywhere = pl.BlockSpec(memory_space=pl.ANY)
         vmem = pl.BlockSpec(memory_space=pltpu.VMEM)

time: 83.4 us -> 79.7 us (0.956)
  Pallas kernels: 82.3 us -> 78.2 us
    pallas_call x1, Pallas kernels: 76.6 us -> 72.4 us  [shards(): pl.pallas_call(functools.partial(main_kernel, (groups, members, rows, wid...]
where the time goes in v2:
time: 79.7 us; the launch traced here: 79 us
  Pallas kernels  78.2 us (98%)
  between operations  0.85 us (1%)
    pallas_call x1, Pallas kernels, shards(): pl.pallas_call(functools.partial(main_kernel, (groups, members, rows, wid...  72.4 us
    pallas_call x1, Pallas kernels, shards(): pl.pallas_call(functools.partial(result_kernel, count), out_shape=results...  5.73 us

profile of v2, /device:TPU:0, one launch (start us, length us, event | category | flops | bytes accessed | tf_op | source)
XLA Modules:
  0.0 79.0 jit_solution(8127733730770330167)
XLA Ops:
  0.7 72.4 %layer.1 = (bf16[1024,768]{1,0:T(8,128)(2,1)}, bf16[832,1024]{1,0:T(8,128)(2,1)}, bf16[832,768]{1,0:T(8,128)(2,1)}, f32[48,768]{1,0:T(8,128)}, f32[48]{0:T(128)}...) custom-call(bf16[1024,768]{1,0:T(8,128)(2,1)} %refs_0_.1, ...), custom_call_target="tpu_custom_call" | custom-call | tf_op jit(solution)/shard_map/layer/pallas_call | solution.py:1511
  73.1 5.7 %results.1 = (bf16[1024,768]{1,0:T(8,128)(2,1)}, f32[1024,768]{1,0:T(8,128)}, f32[48,768]{1,0:T(8,128)}, f32[48]{0:T(128)}, f32[48,768]{1,0:T(8,128)}, /*index=5...) custom-call(bf16[1024,768]{1,0:T(8,128)(2,1)} %get-tuple-element.35., ...), custom_call_target="tpu_custom_call" | custom-call | tf_op jit(solution)/shard_map/results/pallas_call | solution.py:1524
